TPU v7x, 32 devices: a whole 2x2x4 slice. The times are simulated.
32 devices in a mesh: mol: 8 (over z, x), row: 4 (over y, core).
Axes of the slice: x: 2, y: 2, z: 4, core: 2. Of those that a mesh axis runs over, the one named last changes fastest.
Arguments:
- edge_feats: bfloat16 [128, 384, 16], P('mol'), may hold values from -5 to 5
- edge_source: int32 [128, 384], P('mol'), may hold values from 0 to 31, as said below
- edge_target: int32 [128, 384], P('mol'), may hold values from 0 to 31, as said below
- atom_counts: int32 [128], P('mol'), may hold values from 16 to 32, as said below
- edge_counts: int32 [128], P('mol'), may hold values from 192 to 384, as said below
- atom_states: bfloat16 [128, 32, 128], P('mol'), may hold values from -3 to 3
- targets: float32 [128, 12], P('mol'), may hold values from -5 to 5
- label_mask: int32 [128, 12], P('mol'), may hold values from 0 to 1, as said below
- edge_input: float32 [16, 128], replicated, may hold values from -1.5 to 1.5
- edge_input_first: float32 [16, 128], replicated, may hold values from -0.00061035156 to 0.00061035156
- edge_input_second: float32 [16, 128], replicated, may hold values from 7.8125e-10 to 3.125e-09
- edge_output: float32 [128, 16384], P(None, 'row'), may hold values from -0.015625 to 0.015625
- edge_output_first: float32 [128, 16384], P(None, 'row'), may hold values from -6.1035156e-05 to 6.1035156e-05
- edge_output_second: float32 [128, 16384], P(None, 'row'), may hold values from 7.8125e-12 to 3.125e-11
- gated_weights: float32 [2, 128, 384], replicated, may hold values from -0.5 to 0.5
- gated_first: float32 [2, 128, 384], replicated, may hold values from -0.00030517578 to 0.00030517578
- gated_second: float32 [2, 128, 384], replicated, may hold values from 1.953125e-10 to 7.8125e-10
- memory_weights: float32 [384, 512], replicated, may hold values from -0.3125 to 0.3125
- memory_first: float32 [384, 512], replicated, may hold values from -0.00018310547 to 0.00018310547
- memory_second: float32 [384, 512], replicated, may hold values from 7.03125e-11 to 2.8125e-10
- readout_hidden: float32 [256, 128], replicated, may hold values from -0.375 to 0.375
- readout_hidden_first: float32 [256, 128], replicated, may hold values from -0.00061035156 to 0.00061035156
- readout_hidden_second: float32 [256, 128], replicated, may hold values from 7.8125e-10 to 3.125e-09
- readout_final: float32 [128, 12], replicated, may hold values from -0.5 to 0.5
- readout_final_first: float32 [128, 12], replicated, may hold values from -0.0048828125 to 0.0048828125
- readout_final_second: float32 [128, 12], replicated, may hold values from 5e-08 to 2e-07
- bias_vector: float32 [1548], replicated, may hold values from -1 to 1
- bias_first: float32 [1548], replicated, may hold values from -0.0029296875 to 0.0029296875
- bias_second: float32 [1548], replicated, may hold values from 1.953125e-08 to 7.8125e-08
Outputs:
- loss_sum: float32 [], replicated
- label_count: float32 [], replicated
- edge_input_new: float32 [16, 128], replicated
- edge_input_first_new: float32 [16, 128], replicated
- edge_input_second_new: float32 [16, 128], replicated
- edge_input_copy: bfloat16 [16, 128], replicated
- edge_output_new: float32 [128, 16384], P(None, 'row')
- edge_output_first_new: float32 [128, 16384], P(None, 'row')
- edge_output_second_new: float32 [128, 16384], P(None, 'row')
- edge_output_copy: bfloat16 [128, 16384], P(None, 'row')
- gated_new: float32 [2, 128, 384], replicated
- gated_first_new: float32 [2, 128, 384], replicated
- gated_second_new: float32 [2, 128, 384], replicated
- gated_copy: bfloat16 [2, 128, 384], replicated
- memory_new: float32 [384, 512], replicated
- memory_first_new: float32 [384, 512], replicated
- memory_second_new: float32 [384, 512], replicated
- memory_copy: bfloat16 [384, 512], replicated
- readout_hidden_new: float32 [256, 128], replicated
- readout_hidden_first_new: float32 [256, 128], replicated
- readout_hidden_second_new: float32 [256, 128], replicated
- readout_hidden_copy: bfloat16 [256, 128], replicated
- readout_final_new: float32 [128, 12], replicated
- readout_final_first_new: float32 [128, 12], replicated
- readout_final_second_new: float32 [128, 12], replicated
- readout_final_copy: bfloat16 [128, 12], replicated
- bias_new: float32 [1548], replicated
- bias_first_new: float32 [1548], replicated
- bias_second_new: float32 [1548], replicated
- bias_copy: bfloat16 [1548], replicated
Inputs may be any that keep to these rules, and one draw needn't show every extreme that they name: Each molecule's edge_source and edge_target entries lie below its atom count and differ; slots at or past its edge count are not edges. `edge_target`: as for edge_source. `atom_counts`: some molecule has 32 atoms. `edge_counts`: some molecule has 384 edges. `label_mask`: at least one label is present.
All inputs are finite; a program needn't handle non-finite values.
Results may differ from a plain program's by a relative error of at most 0.012.
Values may be sent and summed in bfloat16 or wider, within the bound.
A program may use at most 128 MiB of HBM per device.

v0:
```python
import jax
import jax.numpy as jnp
from jax import lax
from jax.sharding import PartitionSpec as P

LAYERS = 2
ROUNDS = 6
STEP = 10


FULL_PRECISION = lax.Precision.HIGHEST
BETA_ONE = 0.9
BETA_TWO = 0.999
EPSILON = 1e-08
DECAY = 0.01
RATES = (0.25, 0.004, 0.09, 0.05, 0.06, 0.09, 0.2)


def rounded(value):
    return lax.optimization_barrier(value.astype(jnp.bfloat16)).astype(jnp.float32)


def low_value(value):
    return value + lax.stop_gradient(rounded(value) - value)


def product(left, right):
    return jnp.dot(left, right, precision=FULL_PRECISION, preferred_element_type=jnp.float32)


def split_bias(bias_vector, width, inner):
    first = bias_vector[:inner]
    gate_in = bias_vector[inner : inner + 3 * width]
    gate_hid = bias_vector[inner + 3 * width : inner + 6 * width]
    memory = bias_vector[inner + 6 * width : inner + 10 * width]
    readout = bias_vector[inner + 10 * width : inner + 11 * width]
    final = bias_vector[inner + 11 * width :]
    return (first, gate_in, gate_hid, memory, readout, final)


def gated_update(gathered, state, state_reduced, gated_low, bias_in, bias_hid):
    width = state.shape[-1]
    gate_in = product(gathered, gated_low[0]) + bias_in
    gate_hid = product(state_reduced, gated_low[1]) + bias_hid
    reset = jax.nn.sigmoid(gate_in[:, :width] + gate_hid[:, :width])
    update = jax.nn.sigmoid(gate_in[:, width : 2 * width] + gate_hid[:, width : 2 * width])
    candidate = jnp.tanh(gate_in[:, 2 * width :] + reset * gate_hid[:, 2 * width :])
    return (1.0 - update) * candidate + update * state


def readout_loss(
    state,
    memory_low,
    hidden_low,
    final_low,
    bias_memory,
    bias_readout,
    bias_final,
    atom_live,
    targets,
    label_float,
    rounding,
):
    mols, atoms, width = state.shape
    atom_low = rounding(state)
    cell = jnp.zeros((mols, width), jnp.float32)
    memory_low_state = jnp.zeros((mols, width), jnp.float32)
    read_low = jnp.zeros((mols, width), jnp.float32)
    for turn in range(ROUNDS):
        joined = jnp.concatenate([memory_low_state, read_low, memory_low_state], axis=1)
        gates = product(joined, memory_low) + bias_memory
        cell = jax.nn.sigmoid(gates[:, width : 2 * width]) * cell + jax.nn.sigmoid(
            gates[:, :width]
        ) * jnp.tanh(gates[:, 2 * width : 3 * width])
        memory_state = jax.nn.sigmoid(gates[:, 3 * width :]) * jnp.tanh(cell)
        memory_low_state = rounding(memory_state)
        scores = jnp.einsum("mac,mc->ma", atom_low, memory_low_state, precision=FULL_PRECISION)
        scores = jnp.where(atom_live, scores, -1000000000.0)
        weights = jnp.exp(scores - jnp.max(scores, axis=1, keepdims=True))
        weights = weights / jnp.sum(weights, axis=1, keepdims=True)
        read = jnp.einsum("ma,mac->mc", rounding(weights), atom_low, precision=FULL_PRECISION)
        read_low = rounding(read)
    joined = jnp.concatenate([memory_low_state, read_low], axis=1)
    inner = jax.nn.silu(product(joined, hidden_low) + bias_readout)
    predicted = product(rounding(inner), final_low) + bias_final
    return jnp.sum(label_float * (predicted - targets) ** 2)


def adamw(weight, first, second, grad, rate):
    first_new = BETA_ONE * first + (1.0 - BETA_ONE) * grad
    second_new = BETA_TWO * second + (1.0 - BETA_TWO) * grad * grad
    corrected = first_new / (1.0 - BETA_ONE**STEP)
    scaled = jnp.sqrt(second_new / (1.0 - BETA_TWO**STEP))
    weight_new = weight - rate * (corrected / (scaled + EPSILON) + DECAY * weight)
    return (weight_new, first_new, second_new, weight_new.astype(jnp.bfloat16))


def blocked(value):
    size = 4
    return value.reshape((value.shape[0] // size, size) + value.shape[1:])


def shards(
    edge_feats,
    edge_source,
    edge_target,
    atom_counts,
    edge_counts,
    atom_states,
    targets,
    label_mask,
    edge_input,
    edge_input_first,
    edge_input_second,
    edge_output,
    edge_output_first,
    edge_output_second,
    gated_weights,
    gated_first,
    gated_second,
    memory_weights,
    memory_first,
    memory_second,
    readout_hidden,
    readout_hidden_first,
    readout_hidden_second,
    readout_final,
    readout_final_first,
    readout_final_second,
    bias_vector,
    bias_first,
    bias_second,
):
    mols, edge_pad, _ = edge_feats.shape
    atom_pad, width = (atom_states.shape[1], atom_states.shape[2])
    row_count = lax.axis_size("row")
    row_index = lax.axis_index("row")
    local_rows = width // row_count
    inner = edge_input.shape[1]
    slots = jnp.arange(atom_pad, dtype=jnp.int32)
    live = jnp.arange(edge_pad, dtype=jnp.int32)[None, :] < edge_counts[:, None]
    source_onehot = (live[..., None] & (edge_source[..., None] == slots)).astype(jnp.bfloat16)
    target_onehot = (live[..., None] & (edge_target[..., None] == slots)).astype(jnp.float32)
    target_narrow = target_onehot.astype(jnp.bfloat16)
    atom_live = slots[None, :] < atom_counts[:, None]
    label_float = label_mask.astype(jnp.float32)
    bias_parts = split_bias(bias_vector, width, inner)
    edge_in_low = edge_input.astype(jnp.bfloat16)
    edge_out_low = edge_output.astype(jnp.bfloat16)
    gated_low = rounded(gated_weights)

    def flatten(value):
        return value.reshape(mols * atom_pad, width)

    def edge_block(feats):
        before = (
            jnp.einsum("mef,fk->mek", feats, edge_in_low, preferred_element_type=jnp.float32)
            + bias_parts[0]
        )
        hidden = jax.nn.silu(before).astype(jnp.bfloat16)
        matrix = jnp.einsum(
            "mek,kj->mej", hidden, edge_out_low, preferred_element_type=jnp.float32
        ).astype(jnp.bfloat16)
        return (before, hidden, matrix.reshape(feats.shape[0], edge_pad, local_rows, width))

    def message_part(block):
        feats, sending_atoms, receiving_atoms, state_reduced = block
        matrix = edge_block(feats)[2]
        sent_messages = jnp.einsum(
            "gkn,gny->gky", sending_atoms, state_reduced, preferred_element_type=jnp.float32
        ).astype(jnp.bfloat16)
        edge_message = jnp.einsum(
            "merc,mec->mer", matrix, sent_messages, preferred_element_type=jnp.float32
        )
        return jnp.einsum("ykh,yks->yhs", receiving_atoms, edge_message, precision=FULL_PRECISION)

    def message_back(carry, block):
        feats, sending_atoms, receiving_atoms, state_reduced, incoming_gradient = block
        before, hidden, matrix = edge_block(feats)
        sent_messages = jnp.einsum(
            "gkn,gny->gky", sending_atoms, state_reduced, preferred_element_type=jnp.float32
        )
        message_gradient = jnp.einsum(
            "vjl,vli->vji", receiving_atoms, incoming_gradient, preferred_element_type=jnp.float32
        ).astype(jnp.bfloat16)
        sent_gradient = jnp.einsum(
            "merc,mer->mec", matrix, message_gradient, preferred_element_type=jnp.float32
        )
        grad_atoms = jnp.einsum(
            "ikt,ikr->itr",
            sending_atoms.astype(jnp.float32),
            sent_gradient,
            precision=FULL_PRECISION,
        )
        grad_matrix = (
            message_gradient.astype(jnp.float32)[..., None] * sent_messages[:, :, None, :]
        ).astype(jnp.bfloat16)
        grad_matrix = grad_matrix.reshape(-1, local_rows * width)
        grad_hidden = jnp.einsum(
            "ej,kj->ek", grad_matrix, edge_out_low, preferred_element_type=jnp.float32
        )
        flat_before = before.reshape(-1, inner)
        squash = jax.nn.sigmoid(flat_before)
        grad_before = grad_hidden * squash * (1.0 + flat_before * (1.0 - squash))
        flat_feats = feats.reshape(-1, feats.shape[-1]).astype(jnp.float32)
        flat_hidden = hidden.reshape(-1, inner)
        grad_in, grad_edge_bias, grad_out = carry
        carry = (
            grad_in + jnp.einsum("ef,ek->fk", flat_feats, grad_before, precision=FULL_PRECISION),
            grad_edge_bias + jnp.sum(grad_before, axis=0),
            grad_out
            + jnp.einsum("ek,ej->kj", flat_hidden, grad_matrix, preferred_element_type=jnp.float32),
        )
        return (carry, grad_atoms)

    state = atom_states.astype(jnp.float32)
    pullbacks = []
    kept = []
    for layer in range(LAYERS):
        state_reduced = state.astype(jnp.bfloat16)
        portion = lax.map(
            message_part,
            (
                blocked(edge_feats),
                blocked(source_onehot),
                blocked(target_onehot),
                blocked(state_reduced),
            ),
        )
        portion = portion.reshape(mols, atom_pad, local_rows).astype(jnp.bfloat16)
        gathered = lax.all_gather(portion, "row", axis=2, tiled=True)
        new_state, pullback = jax.vjp(
            gated_update,
            flatten(gathered.astype(jnp.float32)),
            flatten(state),
            flatten(state_reduced.astype(jnp.float32)),
            gated_low,
            bias_parts[1],
            bias_parts[2],
        )
        pullbacks.append(pullback)
        kept.append(state_reduced)
        state = new_state.reshape(mols, atom_pad, width)
    local_count = jnp.sum(label_float)
    label_count = lax.psum(local_count, "mol")
    seed = 1.0 / label_count

    def head(final_state, memory_low, hidden_low, final_low, bias_memory, bias_readout, bias_final):
        return readout_loss(
            final_state,
            memory_low,
            hidden_low,
            final_low,
            bias_memory,
            bias_readout,
            bias_final,
            atom_live,
            targets,
            label_float,
            low_value,
        )

    loss_local, head_pullback = jax.vjp(
        head,
        state,
        rounded(memory_weights),
        rounded(readout_hidden),
        rounded(readout_final),
        bias_parts[3],
        bias_parts[4],
        bias_parts[5],
    )
    grad_state, grad_memory, grad_rhidden, grad_rfinal, grad_bmemory, grad_breadout, grad_bfinal = (
        head_pullback(seed)
    )
    grad_gated = jnp.zeros_like(gated_weights)
    grad_bias_in = jnp.zeros_like(bias_parts[1])
    grad_bias_hid = jnp.zeros_like(bias_parts[2])
    carry = (jnp.zeros_like(edge_input), jnp.zeros_like(bias_parts[0]), jnp.zeros_like(edge_output))
    for layer in reversed(range(LAYERS)):
        grad_gathered, grad_prev, grad_prev_low, grad_gated_step, grad_in_step, grad_hid_step = (
            pullbacks[layer](flatten(grad_state))
        )
        grad_gated = grad_gated + grad_gated_step
        grad_bias_in = grad_bias_in + grad_in_step
        grad_bias_hid = grad_bias_hid + grad_hid_step
        incoming_gradient = lax.dynamic_slice_in_dim(
            grad_gathered.reshape(mols, atom_pad, width), row_index * local_rows, local_rows, 2
        ).astype(jnp.bfloat16)
        carry, grad_parts = lax.scan(
            message_back,
            carry,
            (
                blocked(edge_feats),
                blocked(source_onehot),
                blocked(target_narrow),
                blocked(kept[layer]),
                blocked(incoming_gradient),
            ),
        )
        if layer > 0:
            grad_sent_state = lax.psum(
                grad_parts.reshape(mols, atom_pad, width).astype(jnp.bfloat16), "row"
            ).astype(jnp.float32)
            grad_state = (grad_prev + grad_prev_low).reshape(
                mols, atom_pad, width
            ) + grad_sent_state
    share = 1.0 / row_count
    grad_in, grad_edge_bias, grad_out = carry
    shared_bias = (
        jnp.concatenate(
            [
                jnp.zeros_like(grad_edge_bias),
                grad_bias_in,
                grad_bias_hid,
                grad_bmemory,
                grad_breadout,
                grad_bfinal,
            ]
        )
        * share
    )
    grad_bias = shared_bias + jnp.concatenate(
        [grad_edge_bias, jnp.zeros(shared_bias.shape[0] - inner, jnp.float32)]
    )
    summed = lax.psum(
        (
            grad_in,
            grad_gated * share,
            grad_memory * share,
            grad_rhidden * share,
            grad_rfinal * share,
            grad_bias,
            loss_local * share,
        ),
        ("mol", "row"),
    )
    scale = 1.0
    loss_sum = summed[6]
    grad_edge = lax.psum(grad_out, "mol") * scale
    edge_result = adamw(edge_output, edge_output_first, edge_output_second, grad_edge, RATES[1])
    first_result = adamw(
        edge_input, edge_input_first, edge_input_second, summed[0] * scale, RATES[0]
    )
    gated_result = adamw(gated_weights, gated_first, gated_second, summed[1] * scale, RATES[2])
    memory_result = adamw(memory_weights, memory_first, memory_second, summed[2] * scale, RATES[3])
    hidden_result = adamw(
        readout_hidden, readout_hidden_first, readout_hidden_second, summed[3] * scale, RATES[4]
    )
    final_result = adamw(
        readout_final, readout_final_first, readout_final_second, summed[4] * scale, RATES[5]
    )
    bias_result = adamw(bias_vector, bias_first, bias_second, summed[5] * scale, RATES[6])
    return (
        loss_sum,
        label_count,
        first_result[0],
        first_result[1],
        first_result[2],
        first_result[3],
        edge_result[0],
        edge_result[1],
        edge_result[2],
        edge_result[3],
        gated_result[0],
        gated_result[1],
        gated_result[2],
        gated_result[3],
        memory_result[0],
        memory_result[1],
        memory_result[2],
        memory_result[3],
        hidden_result[0],
        hidden_result[1],
        hidden_result[2],
        hidden_result[3],
        final_result[0],
        final_result[1],
        final_result[2],
        final_result[3],
        bias_result[0],
        bias_result[1],
        bias_result[2],
        bias_result[3],
    )


def solution(mesh):
    return jax.shard_map(
        shards,
        mesh=mesh,
        in_specs=(
            P("mol", None, None),
            P("mol", None),
            P("mol", None),
            P("mol"),
            P("mol"),
            P("mol", None, None),
            P("mol", None),
            P("mol", None),
            P(),
            P(),
            P(),
            P(None, "row"),
            P(None, "row"),
            P(None, "row"),
            P(),
            P(),
            P(),
            P(),
            P(),
            P(),
            P(),
            P(),
            P(),
            P(),
            P(),
            P(),
            P(),
            P(),
            P(),
        ),
        out_specs=(
            P(),
            P(),
            P(),
            P(),
            P(),
            P(),
            P(None, "row"),
            P(None, "row"),
            P(None, "row"),
            P(None, "row"),
            P(),
            P(),
            P(),
            P(),
            P(),
            P(),
            P(),
            P(),
            P(),
            P(),
            P(),
            P(),
            P(),
            P(),
            P(),
            P(),
            P(),
            P(),
            P(),
            P(),
        ),
        check_vma=False,
    )
```

profile of v0, /device:TPU:0, one launch (start us, length us, event | category | flops | bytes accessed | tf_op | source)
XLA Modules:
  0.0 807.9 jit_solution(11873292920586826088)
XLA Ops:
  17.1 97.3 %while.51 = (s32[]{:T(128)}, bf16[4,4,32,32]{3,2,1,0:T(8,128)(2,1)S(1)}, f32[4,4,384,32]{2,3,1,0:T(8,128)S(1)}, bf16[4,4,384,16]{2,3,1,0:T(8,128)(2,1)}, bf16[16...) while((s32[]{:T(128)}, ...), condition=%wide.region_1.2_spmd, body=%wide.region_0.1_spmd.sunk | while | flops 1668612096 | bytes 53599332 | solution.py:221
  17.1 7.6 convolution_convert_fusion.11
  65.8 7.5 convolution_convert_fusion.11
  114.6 8.9 %all_gather.6 = bf16[16,32,128]{1,0,2:T(8,128)(2,1)S(1)} all-gather(bf16[16,32,32]{1,0,2:T(8,128)(2,1)S(1)} %bitcast.652), channel_id=1, replica_groups=mesh['mol'=8,'row'=4] {'row'}, dimensions={2}, use_global_device_ids=true | all-gather | bytes 163840 | tf_op jit(solution)/shard_map/all_gather | solution.py:231
  126.6 97.3 %while.52 = (s32[]{:T(128)}, bf16[4,4,32,32]{3,2,1,0:T(8,128)(2,1)S(1)}, f32[4,4,384,32]{2,3,1,0:T(8,128)S(1)}, bf16[4,4,384,16]{2,3,1,0:T(8,128)(2,1)}, bf16[16...) while((s32[]{:T(128)}, ...), condition=%wide.region_3.4_spmd, body=%wide.region_2.3_spmd.sunk | while | flops 1668612096 | bytes 53599332 | solution.py:221
  224.1 7.5 all_gather.7
  267.5 22.7 %psum.71 = f32[]{:T(128)} all-reduce(f32[]{:T(128)} %get-tuple-element.476), channel_id=1, replica_groups=mesh['mol'=8,'row'=4] {'mol'}, use_global_device_ids=true, to_apply=%region_19.20 | all-reduce | flops 1 | bytes 8 | tf_op jit(solution)/shard_map/psum | solution.py:245
  323.3 196.0 %while.54 = (s32[]{:T(128)}, f32[16,128]{1,0:T(8,128)S(1)}, f32[128]{0:T(128)}, f32[128,4096]{1,0:T(8,128)}, bf16[4,4,32,128]{3,2,1,0:T(8,128)(2,1)}, /*index=5*...) while((s32[]{:T(128)}, f32[16,128]{1,0:T(8,128)S(1)}, ...), condition=%wide.region_40.41_spmd.clone, body=%wide.region_38.40_spmd.clone.sunk | while | flops 5002612736 | bytes 176613328 | solution.py:290
  326.0 7.8 multiply_convert_fusion.13
  344.6 8.9 %fusion.610 = f32[128,4096]{1,0:T(8,128)S(1)} fusion(bf16[1536,128]{1,0:T(8,128)(2,1)S(1)} %bitcast.631, bf16[192,8,32,128]{3,2,1,0:T(8,128)(2,1)} %bitcast.627, f32[128,4096]{1,0:T(8,128)S(1)} %copy-done.3, pred[]{:T(512)S(6)} %compare.40), kind=kOutput, calls=%fused_computation.98.clone.1 | convolution fusion | flops 1611661312 | bytes 17170432 | tf_op jit(solution)/shard_map/while/body/eval_jaxpr/ek,ej->kj/dot_general | solution.py:212
  374.9 7.8 multiply_convert_fusion.13
  393.5 8.9 %fusion.610 = f32[128,4096]{1,0:T(8,128)S(1)} fusion(bf16[1536,128]{1,0:T(8,128)(2,1)S(1)} %bitcast.631, bf16[192,8,32,128]{3,2,1,0:T(8,128)(2,1)} %bitcast.627, f32[128,4096]{1,0:T(8,128)S(1)} %copy-done.3, pred[]{:T(512)S(6)} %compare.40), kind=kOutput, calls=%fused_computation.98.clone.1 | convolution fusion | flops 1611661312 | bytes 17170432 | tf_op jit(solution)/shard_map/while/body/eval_jaxpr/ek,ej->kj/dot_general | solution.py:212
  423.9 7.8 multiply_convert_fusion.13
  442.4 8.9 %fusion.610 = f32[128,4096]{1,0:T(8,128)S(1)} fusion(bf16[1536,128]{1,0:T(8,128)(2,1)S(1)} %bitcast.631, bf16[192,8,32,128]{3,2,1,0:T(8,128)(2,1)} %bitcast.627, f32[128,4096]{1,0:T(8,128)S(1)} %copy-done.3, pred[]{:T(512)S(6)} %compare.40), kind=kOutput, calls=%fused_computation.98.clone.1 | convolution fusion | flops 1611661312 | bytes 17170432 | tf_op jit(solution)/shard_map/while/body/eval_jaxpr/ek,ej->kj/dot_general | solution.py:212
  472.8 7.8 multiply_convert_fusion.13
  491.3 8.9 %fusion.610 = f32[128,4096]{1,0:T(8,128)S(1)} fusion(bf16[1536,128]{1,0:T(8,128)(2,1)S(1)} %bitcast.631, bf16[192,8,32,128]{3,2,1,0:T(8,128)(2,1)} %bitcast.627, f32[128,4096]{1,0:T(8,128)S(1)} %copy-done.3, pred[]{:T(512)S(6)} %compare.40), kind=kOutput, calls=%fused_computation.98.clone.1 | convolution fusion | flops 1611661312 | bytes 17170432 | tf_op jit(solution)/shard_map/while/body/eval_jaxpr/ek,ej->kj/dot_general | solution.py:212
  538.3 9.7 %all-reduce.43.cloned.1.call-done = bf16[16,32,128]{2,1,0:T(8,128)(2,1)} async-done(((bf16[16,32,128]{2,1,0:T(8,128)(2,1)}), bf16[16,32,128]{2,1,0:T(8,128)(2,1)}) %all-reduce.43.cloned.1.call-update) | async-done | bytes 131088 | tf_op jit(solution)/shard_map/psum | solution.py:302
  552.6 89.9 %while.53 = (s32[]{:T(128)}, f32[16,128]{1,0:T(8,128)S(1)}, f32[128]{0:T(128)}, f32[128,4096]{1,0:T(8,128)}, bf16[4,4,384,16]{2,1,3,0:T(4,128)(2,1)}, /*index=5*...) while((s32[]{:T(128)}, f32[16,128]{1,0:T(8,128)S(1)}, ...), condition=%wide.region_44.45_spmd, body=%wide.region_42.44_spmd.sunk | while | flops 3297150976 | bytes 69792496 | solution.py:290
  555.5 7.8 multiply_convert_fusion.11
  577.9 7.8 multiply_convert_fusion.11
  600.3 7.8 multiply_convert_fusion.11
  622.7 7.8 multiply_convert_fusion.11
  643.4 40.5 %all-reduce.37 = (f32[]{:T(128)}, f32[16,128]{1,0:T(8,128)S(1)}, f32[128,12]{0,1:T(8,128)S(1)}, f32[1548]{0:T(1024)S(1)}) all-reduce(f32[]{:T(128)S(6)} %mul.1022, f32[16,128]{1,0:T(8,128)S(1)} %get-tuple-element.264, f32[128,12]{0,1:T(8,128)S(1)} %copy-done.199, ...), channel_id=1, replica_groups=mesh['mol'=8,'row'=4] {'mol','row'}, use_global_device_ids=true, to_apply=%region_17.18 | all-reduce | flops 5133 | bytes 41064 | tf_op jit(solution)/shard_map/psum | solution.py:326
  695.9 97.9 %all-reduce.45.cloned.1.call-done = f32[128,4096]{1,0:T(8,128)} async-done(((f32[128,4096]{1,0:T(8,128)}), f32[128,4096]{1,0:T(8,128)}) %all-reduce.45.cloned.1.call-update) | async-done | bytes 2097168 | tf_op jit(solution)/shard_map/psum | solution.py:340
  (910 shorter events, 486.6 us)
Async XLA Ops:
  7.2 540.8 %all-reduce.43.cloned.1.call-start = ((), (), s32[]{:S(2)}) async-start(), calls=%async_computation | async-start | bytes 262144 | tf_op jit(solution)/shard_map/psum | solution.py:302
  17.1 106.8 %copy-start.35 = (f32[2,128,384]{2,1,0:T(8,128)S(1)}, f32[2,128,384]{2,1,0:T(8,128)}, u32[]{:S(2)}) copy-start(f32[2,128,384]{2,1,0:T(8,128)} %param.51) | copy-start | bytes 1179652
  235.1 82.5 %copy-start.1 = (f32[16,32,128]{2,1,0:T(8,128)}, f32[16,32,128]{2,1,0:T(8,128)S(1)}, u32[]{:S(2)}) copy-start(f32[16,32,128]{2,1,0:T(8,128)S(1)} %subtract_add_fusion) | copy-start | bytes 786436
  238.7 77.9 %copy-start.44 = (f32[16,512]{1,0:T(8,128)}, f32[16,512]{1,0:T(8,128)S(1)}, u32[]{:S(2)}) copy-start(f32[16,512]{1,0:T(8,128)S(1)} %convolution_add_fusion.19) | copy-start | bytes 98308
  253.3 47.6 %copy-start.180 = (f32[16]{0:T(128)S(1)}, f32[16]{0:T(128)}, u32[]{:S(2)}) copy-start(f32[16]{0:T(128)} %copy-done.179) | copy-start | bytes 196
  519.6 168.7 %all-reduce.47.cloned.1.call-start = ((), (), s32[]{:S(2)}) async-start(), calls=%async_computation.2 | async-start | bytes 2621440 | tf_op jit(solution)/shard_map/psum | solution.py:326
  552.6 241.2 %all-reduce.45.cloned.1.call-start = ((), (), s32[]{:S(2)}) async-start(), calls=%async_computation.1 | async-start | bytes 4194304 | tf_op jit(solution)/shard_map/psum | solution.py:340
  642.6 41.3 %copy-start.171 = (f32[1548]{0:T(1024)S(1)}, f32[1548]{0:T(1024)}, u32[]{:S(2)}) copy-start(f32[1548]{0:T(1024)} %param.63) | copy-start | bytes 18580
  642.6 41.3 %copy-start.189 = (f32[1548]{0:T(1024)S(1)}, f32[1548]{0:T(1024)}, u32[]{:S(2)}) copy-start(f32[1548]{0:T(1024)} %param.64) | copy-start | bytes 18580
  642.7 41.3 %copy-start.190 = (f32[1548]{0:T(1024)S(1)}, f32[1548]{0:T(1024)}, u32[]{:S(2)}) copy-start(f32[1548]{0:T(1024)} %param.65) | copy-start | bytes 18580
  642.7 41.9 %copy-start.167 = (f32[128,12]{0,1:T(8,128)S(1)}, f32[128,12]{0,1:T(8,128)}, u32[]{:S(2)}) copy-start(f32[128,12]{0,1:T(8,128)} %param.60) | copy-start | bytes 18436
  642.7 41.9 %copy-start.191 = (f32[128,12]{0,1:T(8,128)S(1)}, f32[128,12]{0,1:T(8,128)}, u32[]{:S(2)}) copy-start(f32[128,12]{0,1:T(8,128)} %param.61) | copy-start | bytes 18436
  642.7 41.9 %copy-start.192 = (f32[128,12]{0,1:T(8,128)S(1)}, f32[128,12]{0,1:T(8,128)}, u32[]{:S(2)}) copy-start(f32[128,12]{0,1:T(8,128)} %param.62) | copy-start | bytes 18436
  642.7 42.5 %copy-start.169 = (f32[16,128]{1,0:T(8,128)S(1)}, f32[16,128]{1,0:T(8,128)}, u32[]{:S(2)}) copy-start(f32[16,128]{1,0:T(8,128)} %param.45) | copy-start | bytes 24580
  642.7 42.5 %copy-start.193 = (f32[16,128]{1,0:T(8,128)S(1)}, f32[16,128]{1,0:T(8,128)}, u32[]{:S(2)}) copy-start(f32[16,128]{1,0:T(8,128)} %param.46) | copy-start | bytes 24580
  642.7 42.5 %copy-start.194 = (f32[16,128]{1,0:T(8,128)S(1)}, f32[16,128]{1,0:T(8,128)}, u32[]{:S(2)}) copy-start(f32[16,128]{1,0:T(8,128)} %param.47) | copy-start | bytes 24580
  642.7 45.6 %copy-start.43 = (f32[256,128]{1,0:T(8,128)S(1)}, f32[256,128]{1,0:T(8,128)}, u32[]{:S(2)}) copy-start(f32[256,128]{1,0:T(8,128)} %param.57) | copy-start | bytes 393220
  642.8 45.6 %copy-start.133 = (f32[256,128]{1,0:T(8,128)S(1)}, f32[256,128]{1,0:T(8,128)}, u32[]{:S(2)}) copy-start(f32[256,128]{1,0:T(8,128)} %param.58) | copy-start | bytes 393220
  642.8 45.5 %copy-start.134 = (f32[256,128]{1,0:T(8,128)S(1)}, f32[256,128]{1,0:T(8,128)}, u32[]{:S(2)}) copy-start(f32[256,128]{1,0:T(8,128)} %param.59) | copy-start | bytes 393220
  642.8 47.3 %copy-start.36 = (f32[2,128,384]{2,1,0:T(8,128)S(1)}, f32[2,128,384]{2,1,0:T(8,128)}, u32[]{:S(2)}) copy-start(f32[2,128,384]{2,1,0:T(8,128)} %param.51) | copy-start | bytes 1179652
  642.8 47.3 %copy-start.60 = (f32[2,128,384]{2,1,0:T(8,128)S(1)}, f32[2,128,384]{2,1,0:T(8,128)}, u32[]{:S(2)}) copy-start(f32[2,128,384]{2,1,0:T(8,128)} %param.52) | copy-start | bytes 1179652
  642.8 47.3 %copy-start.61 = (f32[2,128,384]{2,1,0:T(8,128)S(1)}, f32[2,128,384]{2,1,0:T(8,128)}, u32[]{:S(2)}) copy-start(f32[2,128,384]{2,1,0:T(8,128)} %param.53) | copy-start | bytes 1179652
  643.4 49.0 %copy-start.20 = (f32[384,512]{1,0:T(8,128)S(1)}, f32[384,512]{1,0:T(8,128)}, u32[]{:S(2)}) copy-start(f32[384,512]{1,0:T(8,128)} %param.54) | copy-start | bytes 2359300
  692.4 101.4 %copy-start.11 = (f32[128,4096]{1,0:T(8,128)S(1)}, f32[128,4096]{1,0:T(8,128)}, u32[]{:S(2)}) copy-start(f32[128,4096]{1,0:T(8,128)} %param.48) | copy-start | bytes 6291460
  (250 other events, 1620.7 us)
Sparse Core Ops, SparseCore 0:
  519.7 28.2 all-reduce.42
  555.9 132.3 all-reduce.46
  692.9 100.7 all-reduce.44
where the time goes:
time: 817 us; the launch traced here: 808 us
  matrix products  339 us (41%)
  other arithmetic  133 us (16%)
  local copies, waits for them, and re-layouts  126 us (15%)
  waiting for transfers between devices  110 us (13%)
  blocking collectives  79.6 us (10%)
  between operations  18.6 us (2%)
    psum x1, waiting for transfers between devices, shards(): grad_edge = lax.psum(grad_out, 'mol') * scale  97.9 us
    while x124, local copies, waits for them, and re-layouts  94.2 us
    dot_general x12, matrix products, edge_block(): jnp.einsum('mek,kj->mej', hidden, edge_out_low, preferred_element_type=jn...  74.9 us
    convert_element_type x8, other arithmetic, message_back(): grad_matrix = (message_gradient.astype(jnp.float32)[..., None] * sent_mes...  62.6 us
    dot_general x8, matrix products, message_part(): jnp.einsum('merc,mec->mer', matrix, sent_messages, preferred_element_type...  60.1 us
    dot_general x8, matrix products, message_back(): jnp.einsum('ek,ej->kj', flat_hidden, grad_matrix, preferred_element_type=...  53.8 us
    psum x1, blocking collectives, shards(): lax.psum((grad_in, grad_gated * share, grad_memory * share, grad_rhidden...  40.5 us
    dot_general x8, matrix products, message_back(): jnp.einsum('ej,kj->ek', grad_matrix, edge_out_low, preferred_element_type...  39.6 us
  transfers between devices with their start and end apart: 3, of which 3 were waited for; matrix products, arithmetic and copies ran while one was open for 14% of the time, Pallas kernels for 0%

commit v1 on v0

v1 whole, which is shorter than its diff:
```python
import functools

import jax
import jax.numpy as jnp
from jax import lax
from jax.experimental import pallas as pl
from jax.experimental.pallas import tpu as pltpu
from jax.sharding import PartitionSpec as P

LAYERS = 2
ROUNDS = 6
STEP = 10
BETA_ONE = 0.9
BETA_TWO = 0.999
EPSILON = 1e-08
DECAY = 0.01
RATES = (0.25, 0.004, 0.09, 0.05, 0.06, 0.09, 0.2)

MESH = pl.DeviceIdType.MESH
F32 = jnp.float32
BF16 = jnp.bfloat16
GROUP = 8
WIDE = 128


def nn(left, right):
    return lax.dot_general(left, right, (((1,), (0,)), ((), ())), preferred_element_type=F32)


def nt(left, right):
    return lax.dot_general(left, right, (((1,), (1,)), ((), ())), preferred_element_type=F32)


def tn(left, right):
    return lax.dot_general(left, right, (((0,), (0,)), ((), ())), preferred_element_type=F32)


def iota(shape, dim):
    return lax.broadcasted_iota(jnp.int32, shape, dim)


def one_hot(condition):
    return jnp.where(condition, 1.0, 0.0).astype(BF16)


def wide(bias_ref, first, count):
    return jnp.concatenate([bias_ref[first + i : first + i + 1, :] for i in range(count)], axis=1)


def step_kernel(
    ring,
    atom_counts,
    edge_counts,
    feats,
    source,
    target,
    states,
    targets,
    labels,
    edge_in,
    edge_out,
    gated,
    memory,
    hidden_w,
    final_w,
    bias,
    grad_edge,
    grad_in,
    grad_gated,
    grad_memory,
    grad_hidden,
    grad_final,
    grad_bias,
    totals,
    edge_low,
    pairs,
    pair_cols,
    sent,
    turned,
    slope,
    pair_grad,
    lows,
    turned_lows,
    gathered,
    gates,
    state,
    state_grad,
    gate_grad,
    pulled,
    memory_low,
    padded,
    parcels,
    reduce_send,
    reduce_recv,
    send_sem,
    recv_sem,
):
    mols, edges, features = feats.shape
    rows_all, width = states.shape
    atoms = rows_all // mols
    local = width // ring
    groups = mols // GROUP
    span = GROUP * atoms
    half = GROUP * local
    block = rows_all // ring
    n_targets = targets.shape[1]
    me = lax.axis_index("row")

    barrier = pltpu.get_barrier_semaphore()
    for k in range(1, ring):
        pl.semaphore_signal(barrier, inc=1, device_id={"row": lax.rem(me + k, ring)}, device_id_type=MESH)

    for r in range(local):
        edge_low[r * width : (r + 1) * width, :] = edge_out[:, r * width : (r + 1) * width].astype(BF16)
    low_in = edge_in[...].astype(BF16)
    memory_low[...] = memory[...].astype(BF16)

    lane_edge = iota((1, edges), 1)
    row_index = iota((256, edges), 0)
    for m in range(mols):
        pairs[m : m + 1, :] = jnp.where(
            lane_edge < edge_counts[m], source[m : m + 1, :] * atoms + target[m : m + 1, :], -1
        )
    pair_cols[...] = pairs[...].astype(F32).T

    def edge_network(m, carry):
        before = nn(feats[m], low_in) + bias[0:1, :]
        squash = jax.nn.sigmoid(before)
        act = before * squash
        slope[m] = squash + act * (1.0 - squash)
        act = act.astype(BF16)
        pair = pairs[pl.ds(m, 1), :]
        rows = pl.ds(pl.multiple_of(m * atoms, atoms), atoms)
        for part in range(atoms * atoms // 256):
            sums = nn(one_hot(row_index + part * 256 == pair), act).astype(BF16)
            for j in range(256 // atoms):
                a = part * (256 // atoms) + j
                sent[rows, a * width : (a + 1) * width] = sums[j * atoms : (j + 1) * atoms]
        return carry

    lax.fori_loop(0, mols, edge_network, 0)

    order = one_hot(
        (iota((span, span), 1) // atoms == iota((span, span), 0) % GROUP)
        & (iota((span, span), 1) % atoms == iota((span, span), 0) // GROUP)
    )
    order_back = one_hot(
        (iota((span, span), 0) // atoms == iota((span, span), 1) % GROUP)
        & (iota((span, span), 0) % atoms == iota((span, span), 1) // GROUP)
    )
    same_mol = iota((span, half), 0) // atoms == iota((span, half), 1) % GROUP
    same_mol_t = iota((half, span), 0) % GROUP == iota((half, span), 1) // atoms

    def message(layer):
        for g in range(groups):
            lows[layer, g * span : (g + 1) * span, :] = nn(
                order, state_low(layer, g)
            ).astype(BF16)
        low_p = lows[layer]
        turned_lows[:, layer * rows_all : (layer + 1) * rows_all] = low_p.astype(F32).T.astype(BF16)

        def rows_pair(rp, carry):
            t = nt(low_p, edge_low[pl.ds(pl.multiple_of(rp * 2 * width, 2 * width), 2 * width), :])
            for g in range(groups):
                base = (g * LAYERS + layer) * half
                where = pl.ds(pl.multiple_of(base + rp * 16, 16), 16)
                for a in range(atoms):
                    at = g * span + a * GROUP
                    tile = jnp.concatenate([t[at : at + GROUP, :width], t[at : at + GROUP, width:]], axis=0)
                    turned[where, a * width : (a + 1) * width] = tile.astype(BF16)
            return carry

        lax.fori_loop(0, local // 2, rows_pair, 0)
        packed = jnp.zeros((block, WIDE), F32)
        for g in range(groups):
            base = (g * LAYERS + layer) * half
            u = nt(sent[g * span : (g + 1) * span, :], turned[base : base + half, :])
            u = jnp.where(same_mol, u, 0.0).astype(BF16)
            for j in range(span // block):
                slot = g * (span // block) + j
                pick = one_hot(iota((half, WIDE), 1) == slot * local + iota((half, WIDE), 0) // GROUP)
                packed = packed + nn(u[j * block : (j + 1) * block], pick)
        return packed.astype(BF16)

    def state_low(layer, g):
        rows = slice(g * span, (g + 1) * span)
        if layer == 0:
            return states[rows, :]
        return state[layer - 1, rows, :].astype(BF16)

    def exchange(stage):
        copies = []
        for k in range(1, ring):
            copy = pltpu.make_async_remote_copy(
                src_ref=parcels.at[stage, me],
                dst_ref=parcels.at[stage, me],
                send_sem=send_sem.at[stage, k - 1],
                recv_sem=recv_sem.at[stage, k - 1],
                device_id={"row": lax.rem(me + k, ring)},
                device_id_type=MESH,
            )
            copy.start()
            copies.append(copy)
        return copies

    gated_low = [gated[i].astype(BF16) for i in range(2)]
    bias_in = wide(bias, 1, 3)
    bias_hid = wide(bias, 4, 3)
    for layer in range(LAYERS):
        parcels[layer, me] = message(layer)
        if layer == 0:
            pl.semaphore_wait(barrier, ring - 1)
        for copy in exchange(layer):
            copy.wait()
        joined = jnp.concatenate([parcels[layer, q] for q in range(ring)], axis=1)
        for j in range(ring):
            line, column = iota((ring * WIDE, width), 0), iota((ring * WIDE, width), 1)
            pick = one_hot(
                (line % WIDE // local == j) & (line // WIDE == column // local) & (line % local == column % local)
            )
            rows = slice(j * block, (j + 1) * block)
            got = nn(joined, pick).astype(BF16)
            gathered[layer, rows, :] = got
            if layer == 0:
                low = states[rows, :]
                old = low.astype(F32)
            else:
                old = state[layer - 1, rows, :]
                low = old.astype(BF16)
            gate_in = nn(got, gated_low[0]) + bias_in
            gate_hid = nn(low, gated_low[1]) + bias_hid
            reset = jax.nn.sigmoid(gate_in[:, :width] + gate_hid[:, :width])
            update = jax.nn.sigmoid(gate_in[:, width : 2 * width] + gate_hid[:, width : 2 * width])
            third = gate_hid[:, 2 * width :]
            candidate = jnp.tanh(gate_in[:, 2 * width :] + reset * third)
            gates[layer, 0, rows, :] = reset
            gates[layer, 1, rows, :] = update
            gates[layer, 2, rows, :] = candidate
            gates[layer, 3, rows, :] = third
            state[layer, rows, :] = (1.0 - update) * candidate + update * old

    atom_low = state[LAYERS - 1].astype(BF16)
    counts = jnp.zeros((mols, 1), jnp.int32)
    for m in range(mols):
        counts = jnp.where(iota((mols, 1), 0) == m, atom_counts[m], counts)
    lane = iota((mols, rows_all), 1)
    own = (lane // atoms == iota((mols, rows_all), 0)) & (lane % atoms < counts)
    bias_memory = wide(bias, 7, 4)
    zero = jnp.zeros((mols, width), F32)
    cell, mem_low, read_low = zero, zero.astype(BF16), zero.astype(BF16)
    kept = []
    for turn in range(ROUNDS):
        join = jnp.concatenate([mem_low, read_low, mem_low], axis=1)
        z = jnp.broadcast_to(bias_memory, (mols, 4 * width))
        if turn > 0:
            z = nn(join, memory_low[...]) + z
        i = jax.nn.sigmoid(z[:, :width])
        f = jax.nn.sigmoid(z[:, width : 2 * width])
        c = jnp.tanh(z[:, 2 * width : 3 * width])
        o = jax.nn.sigmoid(z[:, 3 * width :])
        before_cell = cell
        cell = f * cell + i * c
        squashed = jnp.tanh(cell)
        mem_low = (o * squashed).astype(BF16)
        scores = jnp.where(own, nt(mem_low, atom_low), -1000000000.0)
        weights = jnp.exp(scores - jnp.max(scores, axis=1, keepdims=True))
        weights = weights / jnp.sum(weights, axis=1, keepdims=True)
        weights_low = weights.astype(BF16)
        read_low = nn(weights_low, atom_low).astype(BF16)
        kept.append((join, i, f, c, o, before_cell, squashed, mem_low, weights, weights_low))
    join = jnp.concatenate([mem_low, read_low], axis=1)
    hidden_low = hidden_w[...].astype(BF16)
    padded[...] = jnp.zeros_like(padded)
    padded[0:width, 0:n_targets] = final_w[...]
    final_low = padded[0:width, :].astype(BF16)
    before = nn(join, hidden_low) + bias[11:12, :]
    squash = jax.nn.sigmoid(before)
    inner = before * squash
    inner_low = inner.astype(BF16)
    padded[width : width + mols, 0:n_targets] = targets[...]
    padded[width + mols : width + 2 * mols, 0:n_targets] = labels[...].astype(F32)
    label = padded[width + mols : width + 2 * mols, :]
    gap = nn(inner_low, final_low) + bias[12:13, :] - padded[width : width + mols, :]
    loss = jnp.sum(label * gap * gap)
    present = jnp.sum(label)
    spot = iota((8, WIDE), 1)
    totals[...] = jnp.where(spot == 0, loss, jnp.where(spot == 1, present, 0.0))
    d_pred = 2.0 * label * gap
    d_pred_low = d_pred.astype(BF16)
    grad_final[...] = tn(d_pred_low, inner_low)
    d_before = nt(d_pred_low, final_low) * (squash + inner * (1.0 - squash))
    d_before_low = d_before.astype(BF16)
    grad_hidden[...] = tn(join, d_before_low)
    grad_bias[...] = jnp.zeros_like(grad_bias)
    grad_bias[11:12, :] = jnp.sum(d_before, axis=0, keepdims=True)
    grad_bias[12:13, :] = jnp.sum(d_pred, axis=0, keepdims=True)
    d_join = nt(d_before_low, hidden_low)
    d_mem, d_read = d_join[:, :width], d_join[:, width:]
    d_cell = zero
    d_bias = jnp.zeros((1, 4 * width), F32)
    lefts, rights, joins, d_gates = [], [], [], []
    for turn in reversed(range(ROUNDS)):
        join, i, f, c, o, before_cell, squashed, mem_low, weights, weights_low = kept[turn]
        d_read_low = d_read.astype(BF16)
        d_weights = nt(d_read_low, atom_low)
        d_scores = weights * (d_weights - jnp.sum(weights * d_weights, axis=1, keepdims=True))
        d_scores_low = d_scores.astype(BF16)
        d_mem = d_mem + nn(d_scores_low, atom_low)
        lefts += [weights_low, d_scores_low]
        rights += [d_read_low, mem_low]
        d_out = d_mem * squashed
        d_cell = d_cell + d_mem * o * (1.0 - squashed * squashed)
        d_z = jnp.concatenate(
            [
                d_cell * c * i * (1.0 - i),
                d_cell * before_cell * f * (1.0 - f),
                d_cell * i * (1.0 - c * c),
                d_out * o * (1.0 - o),
            ],
            axis=1,
        )
        d_cell = d_cell * f
        d_bias = d_bias + jnp.sum(d_z, axis=0, keepdims=True)
        d_z_low = d_z.astype(BF16)
        if turn > 0:
            joins.append(join)
            d_gates.append(d_z_low)
            d_join = nt(d_z_low, memory_low[...])
            d_mem = d_join[:, :width] + d_join[:, 2 * width :]
            d_read = d_join[:, width : 2 * width]
    grad_memory[...] = tn(jnp.concatenate(joins, axis=0), jnp.concatenate(d_gates, axis=0))
    for i in range(4):
        grad_bias[7 + i : 8 + i, :] = d_bias[:, i * width : (i + 1) * width]
    state_grad[...] = tn(jnp.concatenate(lefts, axis=0), jnp.concatenate(rights, axis=0))

    def gated_back(layer):
        bias_parts = [jnp.zeros((1, 3 * width), F32) for _ in range(2)]
        for j in range(ring):
            rows = slice(j * block, (j + 1) * block)
            reset, update = gates[layer, 0, rows, :], gates[layer, 1, rows, :]
            candidate, third = gates[layer, 2, rows, :], gates[layer, 3, rows, :]
            old = states[rows, :].astype(F32) if layer == 0 else state[layer - 1, rows, :]
            grad = state_grad[rows, :]
            d_candidate = grad * (1.0 - update) * (1.0 - candidate * candidate)
            d_update = grad * (old - candidate) * update * (1.0 - update)
            d_reset = d_candidate * third * reset * (1.0 - reset)
            d_in = jnp.concatenate([d_reset, d_update, d_candidate], axis=1)
            d_hid = jnp.concatenate([d_reset, d_update, d_candidate * reset], axis=1)
            bias_parts[0] = bias_parts[0] + jnp.sum(d_in, axis=0, keepdims=True)
            bias_parts[1] = bias_parts[1] + jnp.sum(d_hid, axis=0, keepdims=True)
            d_in_low, d_hid_low = d_in.astype(BF16), d_hid.astype(BF16)
            gate_grad[0, rows, :] = d_in_low
            gate_grad[1, rows, :] = d_hid_low
            pulled[layer, rows, :] = nt(d_in_low, gated_low[0]).astype(BF16)
            if layer > 0:
                state_grad[rows, :] = grad * update + nt(d_hid_low, gated_low[1])
        low = states[...] if layer == 0 else state[layer - 1].astype(BF16)
        d_first = tn(gathered[layer], gate_grad[0])
        d_second = tn(low, gate_grad[1])
        if layer == LAYERS - 1:
            grad_gated[0], grad_gated[1] = d_first, d_second
        else:
            grad_gated[0] += d_first
            grad_gated[1] += d_second
        for s in range(2):
            for i in range(3):
                at = 1 + 3 * s + i
                grad_bias[at : at + 1, :] += bias_parts[s][:, i * width : (i + 1) * width]

    pick_t = one_hot(iota((half, width), 1) == me * local + iota((half, width), 0) // GROUP)
    pick_n = one_hot(iota((width, half), 0) == me * local + iota((width, half), 1) // GROUP)

    def message_back(layer, gt):
        for g in range(groups):
            wide_grad = jnp.where(same_mol_t, nt(pick_t, pulled[layer, g * span : (g + 1) * span, :]), 0.0).astype(BF16)

            def atoms_pair(ap, carry, g=g, wide_grad=wide_grad):
                columns = pl.ds(pl.multiple_of(ap * 2 * width, 2 * width), 2 * width)
                x = nn(wide_grad, sent[g * span : (g + 1) * span, columns])
                where = pl.ds(pl.multiple_of(layer * rows_all + g * span + ap * 16, 16), 16)
                for r in range(local):
                    at = r * GROUP
                    tile = jnp.concatenate([x[at : at + GROUP, :width], x[at : at + GROUP, width:]], axis=0)
                    gt[where, r * width : (r + 1) * width] = tile.astype(BF16)
                return carry

            lax.fori_loop(0, atoms // 2, atoms_pair, 0)

    def run(gt):
        for layer in reversed(range(LAYERS)):
            gated_back(layer)
            message_back(layer, gt)
            if layer > 0:
                back = nn(gt[layer * rows_all : (layer + 1) * rows_all, :], edge_low[...]).astype(BF16)
                for g in range(groups):
                    reduce_send[g * span : (g + 1) * span, :] = nn(order_back, back[g * span : (g + 1) * span]).astype(BF16)
                copies = []
                for k in range(1, ring):
                    peer = lax.rem(me + k, ring)
                    copy = pltpu.make_async_remote_copy(
                        src_ref=reduce_send.at[pl.ds(pl.multiple_of(peer * block, block), block), :],
                        dst_ref=reduce_recv.at[k - 1],
                        send_sem=send_sem.at[LAYERS + 1, k - 1],
                        recv_sem=recv_sem.at[LAYERS + 1, k - 1],
                        device_id={"row": peer},
                        device_id_type=MESH,
                    )
                    copy.start()
                    copies.append(copy)
                for copy in copies:
                    copy.wait()
                total = reduce_send[pl.ds(pl.multiple_of(me * block, block), block), :].astype(F32)
                for k in range(ring - 1):
                    total = total + reduce_recv[k].astype(F32)
                parcels[LAYERS, me] = total.astype(BF16)
                for copy in exchange(LAYERS):
                    copy.wait()
                for j in range(ring):
                    rows = slice(j * block, (j + 1) * block)
                    state_grad[rows, :] += parcels[LAYERS, j].astype(F32)

        def out_weights(rp, carry):
            columns = pl.ds(pl.multiple_of(rp * 2 * width, 2 * width), 2 * width)
            grad_edge[columns, :] = nn(turned_lows[...], gt[:, columns]).T.astype(BF16)
            return carry

        lax.fori_loop(0, local // 2, out_weights, 0)

    pl.run_scoped(run, pltpu.VMEM((LAYERS * rows_all, local * width), BF16))

    for g in range(groups):
        wide_grad = jnp.concatenate(
            [
                jnp.where(same_mol, nn(pulled[layer, g * span : (g + 1) * span, :], pick_n), 0.0).astype(BF16)
                for layer in range(LAYERS)
            ],
            axis=1,
        )

        def pair_back(ap, carry, g=g, wide_grad=wide_grad):
            columns = pl.ds(pl.multiple_of(ap * 2 * width, 2 * width), 2 * width)
            x = nn(wide_grad, turned[g * LAYERS * half : (g + 1) * LAYERS * half, columns]).astype(BF16)
            for s in range(2):
                where = pl.ds(pl.multiple_of((ap * 2 + s) * atoms, atoms), atoms)
                for m in range(GROUP):
                    pair_grad[g * GROUP + m, where, :] = x[m * atoms : (m + 1) * atoms, s * width : (s + 1) * width]
            return carry

        lax.fori_loop(0, atoms // 2, pair_back, 0)

    lane_pair = iota((edges, atoms * atoms), 1).astype(F32)
    lane_mol = iota((edges, mols), 1)

    def edge_back(m, carry):
        total_in, total_bias = carry
        column = jnp.sum(jnp.where(lane_mol == m, pair_cols[...], 0.0), axis=1, keepdims=True)
        d_act = nn(one_hot(lane_pair == column), pair_grad[m])
        d_first = d_act * slope[m]
        total_in = total_in + tn(feats[m], d_first.astype(BF16))
        return (total_in, total_bias + jnp.sum(d_first, axis=0, keepdims=True))

    total_in, total_bias = lax.fori_loop(
        0, mols, edge_back, (jnp.zeros((features, width), F32), jnp.zeros((1, width), F32))
    )
    grad_in[...] = total_in
    grad_bias[0:1, :] = total_bias


def adamw(weight, first, second, grad, rate):
    first_new = BETA_ONE * first + (1.0 - BETA_ONE) * grad
    second_new = BETA_TWO * second + (1.0 - BETA_TWO) * grad * grad
    corrected = first_new / (1.0 - BETA_ONE**STEP)
    scaled = jnp.sqrt(second_new / (1.0 - BETA_TWO**STEP))
    weight_new = weight - rate * (corrected / (scaled + EPSILON) + DECAY * weight)
    return (weight_new, first_new, second_new, weight_new.astype(BF16))


def shards(
    edge_feats,
    edge_source,
    edge_target,
    atom_counts,
    edge_counts,
    atom_states,
    targets,
    label_mask,
    edge_input,
    edge_input_first,
    edge_input_second,
    edge_output,
    edge_output_first,
    edge_output_second,
    gated_weights,
    gated_first,
    gated_second,
    memory_weights,
    memory_first,
    memory_second,
    readout_hidden,
    readout_hidden_first,
    readout_hidden_second,
    readout_final,
    readout_final_first,
    readout_final_second,
    bias_vector,
    bias_first,
    bias_second,
):
    mols, edges, features = edge_feats.shape
    atoms, width = atom_states.shape[1:]
    ring = lax.axis_size("row")
    local = width // ring
    rows_all = mols * atoms
    block = rows_all // ring
    n_bias = bias_vector.shape[0]
    n_targets = targets.shape[1]
    bias_rows = jnp.pad(bias_vector, (0, 16 * WIDE - n_bias)).reshape(16, WIDE)
    vmem = pl.BlockSpec(memory_space=pltpu.VMEM)
    smem = pl.BlockSpec(memory_space=pltpu.SMEM)
    shape = jax.ShapeDtypeStruct
    grad_edge, grad_in, grad_gated, grad_memory, grad_hidden, grad_final, grad_bias, totals = pl.pallas_call(
        functools.partial(step_kernel, ring),
        out_shape=[
            shape((local * width, width), BF16),
            shape((features, width), F32),
            shape((2, width, 3 * width), F32),
            shape((3 * width, 4 * width), F32),
            shape((2 * width, width), F32),
            shape((WIDE, width), F32),
            shape((16, WIDE), F32),
            shape((8, WIDE), F32),
        ],
        in_specs=[smem, smem] + [vmem] * 13,
        out_specs=[vmem] * 8,
        scratch_shapes=[
            pltpu.VMEM((local * width, width), BF16),
            pltpu.VMEM((mols, edges), jnp.int32),
            pltpu.VMEM((edges, mols), F32),
            pltpu.VMEM((rows_all, atoms * width), BF16),
            pltpu.VMEM((mols // GROUP * LAYERS * GROUP * local, atoms * width), BF16),
            pltpu.VMEM((mols, edges, width), F32),
            pltpu.VMEM((mols, atoms * atoms, width), BF16),
            pltpu.VMEM((LAYERS, rows_all, width), BF16),
            pltpu.VMEM((width, LAYERS * rows_all), BF16),
            pltpu.VMEM((LAYERS, rows_all, width), BF16),
            pltpu.VMEM((LAYERS, 4, rows_all, width), F32),
            pltpu.VMEM((LAYERS, rows_all, width), F32),
            pltpu.VMEM((rows_all, width), F32),
            pltpu.VMEM((2, rows_all, 3 * width), BF16),
            pltpu.VMEM((LAYERS, rows_all, width), BF16),
            pltpu.VMEM((3 * width, 4 * width), BF16),
            pltpu.VMEM((width + 2 * mols, WIDE), F32),
            pltpu.VMEM((LAYERS + 1, ring, block, WIDE), BF16),
            pltpu.VMEM((rows_all, width), BF16),
            pltpu.VMEM((ring - 1, block, width), BF16),
            pltpu.SemaphoreType.DMA((LAYERS + 2, ring - 1)),
            pltpu.SemaphoreType.DMA((LAYERS + 2, ring - 1)),
        ],
        compiler_params=pltpu.CompilerParams(
            collective_id=0, has_side_effects=True, vmem_limit_bytes=60 * 1024 * 1024
        ),
    )(
        atom_counts,
        edge_counts,
        edge_feats,
        edge_source,
        edge_target,
        atom_states.reshape(rows_all, width),
        targets,
        label_mask,
        edge_input,
        edge_output,
        gated_weights,
        memory_weights,
        readout_hidden,
        readout_final,
        bias_rows,
    )
    share = 1.0 / ring
    spread = jnp.where(jnp.arange(16)[:, None] == 0, 1.0, share)
    totals = lax.psum(totals, "mol")
    loss_sum, label_count = totals[0, 0], totals[0, 1]
    scale = 1.0 / label_count
    grad_in, grad_gated, grad_memory, grad_hidden, grad_final, grad_bias = lax.psum(
        (
            grad_in,
            grad_gated * share,
            grad_memory * share,
            grad_hidden * share,
            grad_final * share,
            grad_bias * spread,
        ),
        ("mol", "row"),
    )
    grad_edge = lax.psum(grad_edge.astype(F32), "mol").reshape(local, width, width)
    grad_edge = grad_edge.transpose(1, 0, 2).reshape(width, local * width)
    grads = (
        grad_in,
        grad_edge,
        grad_gated,
        grad_memory,
        grad_hidden,
        grad_final.T[:, :n_targets],
        grad_bias.reshape(-1)[:n_bias],
    )
    kept = (
        (edge_input, edge_input_first, edge_input_second),
        (edge_output, edge_output_first, edge_output_second),
        (gated_weights, gated_first, gated_second),
        (memory_weights, memory_first, memory_second),
        (readout_hidden, readout_hidden_first, readout_hidden_second),
        (readout_final, readout_final_first, readout_final_second),
        (bias_vector, bias_first, bias_second),
    )
    outs = (loss_sum, label_count)
    for (weight, first, second), grad, rate in zip(kept, grads, RATES):
        outs += adamw(weight, first, second, grad * scale, rate)
    return outs


def solution(mesh):
    cut = P(None, "row")
    per_mol = (P("mol", None, None), P("mol", None), P("mol", None), P("mol"), P("mol"), P("mol", None, None))
    per_mol += (P("mol", None), P("mol", None))
    return jax.shard_map(
        shards,
        mesh=mesh,
        in_specs=per_mol + (P(),) * 3 + (cut,) * 3 + (P(),) * 15,
        out_specs=(P(),) * 6 + (cut,) * 4 + (P(),) * 20,
        check_vma=False,
    )
```

time: 817 us -> 272 us (0.33)
  matrix products: 339 us -> 0 us
  local copies, waits for them, and re-layouts: 126 us -> 6.74 us
  other arithmetic: 133 us -> 21.9 us
  waiting for transfers between devices: 110 us -> 0.02 us
  Pallas kernels: 0 us -> 87.1 us
  blocking collectives: 79.6 us -> 140 us
    dot_general x149 -> x0, matrix products: 339 us -> none  [the longest x12 74.9 us: edge_block(): jnp.einsum('mek,kj->mej', hidden, edge_out_low, preferred_element_type=jn...]
    psum x3 -> x1, waiting for transfers between devices: 110 us -> 0.01 us  [shards(): lax.psum((grad_in, grad_gated * share, grad_memory * share, grad_hidden *...]
    while x124 -> x0, local copies, waits for them, and re-layouts: 94.2 us -> none
    pallas_call x0 -> x1, Pallas kernels: none -> 87.1 us  [shards(): pl.pallas_call(functools.partial(step_kernel, ring), out_shape=[shape((lo...]
    psum x2, blocking collectives: 63.2 us -> 140 us  [the longest x1 97.8 us: shards(): totals = lax.psum(totals, 'mol')]
    convert_element_type x36 -> x7, other arithmetic: 85 us -> 14.6 us  [adamw(): return (weight_new, first_new, second_new, weight_new.astype(BF16))]
    reduce_sum x30 -> x0, other arithmetic: 20 us -> none  [the longest x12 11.2 us: readout_loss(): weights = jnp.exp(scores - jnp.max(scores, axis=1, keepdims=True))]
    all_gather x2 -> x0, blocking collectives: 16.4 us -> none  [shards(): gathered = lax.all_gather(portion, 'row', axis=2, tiled=True)]
  transfers between devices with their start and end apart: 3 -> 1, of which waited for: 3 -> 0; matrix products, arithmetic and copies ran while one was open for 14% -> 3% of each run, Pallas kernels for 0% -> 0%
where the time goes in v1:
time: 272 us; the launch traced here: 271 us
  blocking collectives  140 us (51%)
  Pallas kernels  87.1 us (32%)
  other arithmetic  21.9 us (8%)
  between operations  14.9 us (5%)
  local copies, waits for them, and re-layouts  6.74 us (2%)
    psum x1, blocking collectives, shards(): totals = lax.psum(totals, 'mol')  97.8 us
    pallas_call x1, Pallas kernels, shards(): pl.pallas_call(functools.partial(step_kernel, ring), out_shape=[shape((lo...  87.1 us
    psum x1, blocking collectives, shards(): lax.psum((grad_in, grad_gated * share, grad_memory * share, grad_hidden *...  42.5 us
    convert_element_type x7, other arithmetic, adamw(): return (weight_new, first_new, second_new, weight_new.astype(BF16))  14.6 us
  transfers between devices with their start and end apart: 1, of which 0 were waited for; matrix products, arithmetic and copies ran while one was open for 3% of the time, Pallas kernels for 0%

profile of v1, /device:TPU:0, one launch (start us, length us, event | category | flops | bytes accessed | tf_op | source)
XLA Modules:
  0.0 271.0 jit_solution(16320125313622160932)
XLA Ops:
  7.2 0.0 all-reduce.7.cloned.1.call-start
  7.2 2.3 copy.59.feats
  9.6 1.4 copy.60.final_w
  11.0 1.3 pad_bitcast_fusion.bias
  12.3 87.1 %shard_map.508 = (bf16[4096,128]{1,0:T(8,128)(2,1)}, f32[16,128]{1,0:T(8,128)}, f32[2,128,384]{2,1,0:T(8,128)}, f32[384,512]{1,0:T(8,128)}, f32[256,128]{1,0:T(8...) custom-call(s32[16]{0:T(128)} %atom_counts.1, s32[16]{0:T(128)} %edge_counts.1, ...), custom_call_target="tpu_custom_call" | custom-call | tf_op jit(solution)/shard_map/pallas_call | solution.py:521
  99.5 1.9 broadcast_multiply_fusion.2
  101.4 2.1 broadcast_multiply_fusion.1
  103.4 0.7 broadcast_multiply_fusion.3
  104.1 0.6 multiply_bitcast_fusion
  104.7 0.0 all-reduce.7.cloned.1.call-update
  104.8 97.8 %all-reduce.8 = (f32[8,128]{1,0:T(8,128)S(1)}, f32[4096,128]{1,0:T(8,128)}) all-reduce(f32[8,128]{1,0:T(8,128)S(1)} %copy-done.20, bf16[4096,128]{1,0:T(8,128)(2,1)S(1)} %copy-done.5), channel_id=1, replica_groups=mesh['mol'=8,'row'=4] {'mol'}, use_global_device_ids=true, to_apply=%region_0.1 | all-reduce | flops 525312 | bytes 3153920 | tf_op jit(solution)/shard_map/psum | solution.py:581
  202.6 0.6 fusion.23
  203.9 1.9 broadcast_multiply_fusion
  205.8 0.3 copy-done
  206.1 0.6 copy-done.2
  206.8 4.1 %fusion.18 = (bf16[128,4096]{1,0:T(8,128)(2,1)}, f32[128,4096]{1,0:T(8,128)}, f32[128,4096]{1,0:T(8,128)}, f32[128,4096]{1,0:T(8,128)}) fusion(f32[128,4096]{1,0:T(8,128)S(1)} %copy-done, f32[32,16,8,128]{3,2,1,0:T(8,128)S(1)} %bitcast.20, f32[128,4096]{1,0:T(8,128)S(1)} %copy-done.2, f32[128,4096]{1,0:T(8,128)S(1)} %copy-done.3), kind=kLoop, calls=%fused_computation.44 | loop fusion | flops 8388608 | bytes 15728640 | tf_op jit(solution)/shard_map/convert_element_type | solution.py:475
  210.9 0.1 multiply_bitcast_fusion.1
  211.0 42.5 %all-reduce.1 = (f32[16,128]{1,0:T(8,128)S(1)}, f32[2048]{0:T(1024)S(1)}) all-reduce(f32[16,128]{1,0:T(8,128)} %get-tuple-element.39, f32[2048]{0:T(1024)S(1)} %multiply_bitcast_fusion.1), channel_id=1, replica_groups=mesh['mol'=8,'row'=4] {'mol','row'}, use_global_device_ids=true, to_apply=%region_1.2 | all-reduce | flops 4096 | bytes 32768 | tf_op jit(solution)/shard_map/psum | solution.py:584
  253.5 1.3 fusion.21
  254.8 1.3 fusion.8
  256.2 2.5 fusion.16
  258.8 3.2 %fusion.14 = (bf16[384,512]{1,0:T(8,128)(2,1)}, f32[384,512]{1,0:T(8,128)}, f32[384,512]{1,0:T(8,128)}, f32[384,512]{1,0:T(8,128)}) fusion(f32[384,512]{1,0:T(8,128)S(1)} %copy-done.1, f32[384,512]{1,0:T(8,128)} %get-tuple-element.49, f32[]{:T(128)S(6)} %div.108, f32[384,512]{1,0:T(8,128)S(1)} %copy-done.6, f32[384,512]{1,0:T(8,128)S(1)} %copy-done.7), kind=kLoop, calls=%fused_computation.42 | loop fusion | flops 3342336 | bytes 5898244 | tf_op jit(solution)/shard_map/convert_element_type | solution.py:475
  262.0 0.8 fusion.12
  262.9 1.3 fusion.10
  (42 shorter events, 0.1 us)
Async XLA Ops:
  7.2 249.0 %all-reduce.7.cloned.1.call-start = ((), (), s32[]{:S(2)}) async-start(), calls=%async_computation | async-start | bytes 2752512 | tf_op jit(solution)/shard_map/psum | solution.py:584
  99.5 4.0 %copy-start.12 = (f32[256,128]{1,0:T(8,128)S(1)}, f32[256,128]{1,0:T(8,128)}, u32[]{:S(2)}) copy-start(f32[256,128]{1,0:T(8,128)} %get-tuple-element.43) | copy-start | bytes 393220
  99.5 4.6 %copy-start.13 = (f32[128,128]{1,0:T(8,128)S(1)}, f32[128,128]{1,0:T(8,128)}, u32[]{:S(2)}) copy-start(f32[128,128]{1,0:T(8,128)} %get-tuple-element.44) | copy-start | bytes 196612
  99.5 5.3 %copy-start.5 = (bf16[4096,128]{1,0:T(8,128)(2,1)S(1)}, bf16[4096,128]{1,0:T(8,128)(2,1)}, u32[]{:S(2)}) copy-start(bf16[4096,128]{1,0:T(8,128)(2,1)} %get-tuple-element.40) | copy-start | bytes 3145732
  99.5 5.3 %copy-start.20 = (f32[8,128]{1,0:T(8,128)S(1)}, f32[8,128]{1,0:T(8,128)}, u32[]{:S(2)}) copy-start(f32[8,128]{1,0:T(8,128)} %get-tuple-element.38) | copy-start | bytes 12292
  104.7 101.0 %copy-start.3 = (f32[128,4096]{1,0:T(8,128)S(1)}, f32[128,4096]{1,0:T(8,128)}, u32[]{:S(2)}) copy-start(f32[128,4096]{1,0:T(8,128)} %param.42) | copy-start | bytes 6291460
  203.8 2.3 copy-start
  203.9 2.9 %copy-start.2 = (f32[128,4096]{1,0:T(8,128)S(1)}, f32[128,4096]{1,0:T(8,128)}, u32[]{:S(2)}) copy-start(f32[128,4096]{1,0:T(8,128)} %param.41) | copy-start | bytes 6291460
  206.8 4.1 %copy-start.19 = (f32[16,128]{1,0:T(8,128)S(1)}, f32[16,128]{1,0:T(8,128)}, u32[]{:S(2)}) copy-start(f32[16,128]{1,0:T(8,128)} %get-tuple-element.45) | copy-start | bytes 24580
  206.8 46.7 %copy-start.14 = (f32[16,128]{1,0:T(8,128)S(1)}, f32[16,128]{1,0:T(8,128)}, u32[]{:S(2)}) copy-start(f32[16,128]{1,0:T(8,128)} %edge_in.1) | copy-start | bytes 24580
  206.8 48.1 %copy-start.16 = (f32[1548]{0:T(1024)S(1)}, f32[1548]{0:T(1024)}, u32[]{:S(2)}) copy-start(f32[1548]{0:T(1024)} %param.55) | copy-start | bytes 18580
  206.8 49.4 %copy-start.4 = (f32[2,128,384]{2,1,0:T(8,128)S(1)}, f32[2,128,384]{2,1,0:T(8,128)}, u32[]{:S(2)}) copy-start(f32[2,128,384]{2,1,0:T(8,128)} %gated.1) | copy-start | bytes 1179652
  210.9 47.8 %copy-start.1 = (f32[384,512]{1,0:T(8,128)S(1)}, f32[384,512]{1,0:T(8,128)}, u32[]{:S(2)}) copy-start(f32[384,512]{1,0:T(8,128)} %memory.1) | copy-start | bytes 2359300
  210.9 47.8 %copy-start.6 = (f32[384,512]{1,0:T(8,128)S(1)}, f32[384,512]{1,0:T(8,128)}, u32[]{:S(2)}) copy-start(f32[384,512]{1,0:T(8,128)} %param.47) | copy-start | bytes 2359300
  210.9 47.8 %copy-start.7 = (f32[384,512]{1,0:T(8,128)S(1)}, f32[384,512]{1,0:T(8,128)}, u32[]{:S(2)}) copy-start(f32[384,512]{1,0:T(8,128)} %param.48) | copy-start | bytes 2359300
  258.7 3.3 %copy-start.8 = (f32[256,128]{1,0:T(8,128)S(1)}, f32[256,128]{1,0:T(8,128)}, u32[]{:S(2)}) copy-start(f32[256,128]{1,0:T(8,128)} %hidden_w.1) | copy-start | bytes 393220
  258.7 3.3 %copy-start.9 = (f32[256,128]{1,0:T(8,128)S(1)}, f32[256,128]{1,0:T(8,128)}, u32[]{:S(2)}) copy-start(f32[256,128]{1,0:T(8,128)} %param.50) | copy-start | bytes 393220
  258.7 3.3 %copy-start.10 = (f32[256,128]{1,0:T(8,128)S(1)}, f32[256,128]{1,0:T(8,128)}, u32[]{:S(2)}) copy-start(f32[256,128]{1,0:T(8,128)} %param.51) | copy-start | bytes 393220
  258.7 3.3 %copy-start.11 = (f32[256,128]{1,0:T(8,128)S(1)}, f32[256,128]{1,0:T(8,128)}, u32[]{:S(2)}) copy-start(f32[256,128]{1,0:T(8,128)} %get-tuple-element.50) | copy-start | bytes 393220
  258.7 4.1 %copy-start.15 = (f32[128,12]{0,1:T(8,128)S(1)}, f32[128,12]{0,1:T(8,128)}, u32[]{:S(2)}) copy-start(f32[128,12]{0,1:T(8,128)} %param.52) | copy-start | bytes 18436
  258.8 4.1 %copy-start.17 = (f32[128,12]{0,1:T(8,128)S(1)}, f32[128,12]{0,1:T(8,128)}, u32[]{:S(2)}) copy-start(f32[128,12]{0,1:T(8,128)} %param.53) | copy-start | bytes 18436
  258.8 4.1 %copy-start.18 = (f32[128,12]{0,1:T(8,128)S(1)}, f32[128,12]{0,1:T(8,128)}, u32[]{:S(2)}) copy-start(f32[128,12]{0,1:T(8,128)} %param.54) | copy-start | bytes 18436
Sparse Core Ops, SparseCore 0:
  104.9 142.6 all-reduce.6

commit v2 on v1

--- a/solution.py
+++ b/solution.py
@@ -47,8 +47,27 @@
     return jnp.concatenate([bias_ref[first + i : first + i + 1, :] for i in range(count)], axis=1)
 
 
+def round_up(value, unit):
+    return -(-value // unit) * unit
+
+
+class Plan:
+    def __init__(self, ring, peers, width, local, features):
+        unit = 16 * peers
+        self.edge = local * width
+        self.edge_part = self.edge // peers
+        self.final_at = 12 * width + 2 * width
+        self.head = round_up(-(-(self.final_at + 16) // ring), unit)
+        self.head_part = self.head // peers
+        self.bias_at = 6 * width
+        self.rest_own = round_up(-(-(self.bias_at + 16) // ring), 16)
+        self.rest = round_up(self.rest_own + features + 16, unit)
+        self.rest_part = self.rest // peers
+
+
 def step_kernel(
     ring,
+    peers,
     atom_counts,
     edge_counts,
     feats,
@@ -64,13 +83,9 @@
     hidden_w,
     final_w,
     bias,
-    grad_edge,
-    grad_in,
-    grad_gated,
-    grad_memory,
-    grad_hidden,
-    grad_final,
-    grad_bias,
+    edge_sum,
+    head_sum,
+    rest_sum,
     totals,
     edge_low,
     pairs,
@@ -92,10 +107,26 @@
     parcels,
     reduce_send,
     reduce_recv,
+    grad_gated,
+    grad_bias,
+    totals_all,
+    edge_part,
+    edge_recv,
+    edge_all,
+    head_part,
+    head_recv,
+    head_all,
+    rest_full,
+    rest_part,
+    rest_recv,
+    rest_all,
     send_sem,
     recv_sem,
+    far_send,
+    far_recv,
+    gt,
 ):
-    mols, edges, features = feats.shape
+    mols, features, edges = feats.shape
     rows_all, width = states.shape
     atoms = rows_all // mols
     local = width // ring
@@ -105,10 +136,44 @@
     block = rows_all // ring
     n_targets = targets.shape[1]
     me = lax.axis_index("row")
+    place = lax.axis_index("mol")
+    plan = Plan(ring, peers, width, local, features)
+    started = []
+
+    def rows16(start, count):
+        return pl.ds(pl.multiple_of(start, 16), count)
+
+    def far_copy(stage, index, peer, source_ref, target_ref):
+        copy = pltpu.make_async_remote_copy(
+            src_ref=source_ref,
+            dst_ref=target_ref,
+            send_sem=far_send.at[stage, index],
+            recv_sem=far_recv.at[stage, index],
+            device_id={"mol": peer},
+            device_id_type=MESH,
+        )
+        copy.start()
+        started.append(copy)
+        return copy
+
+    def row_copy(stage, k, source_ref, target_ref):
+        copy = pltpu.make_async_remote_copy(
+            src_ref=source_ref,
+            dst_ref=target_ref,
+            send_sem=send_sem.at[stage, k - 1],
+            recv_sem=recv_sem.at[stage, k - 1],
+            device_id={"row": lax.rem(me + k, ring)},
+            device_id_type=MESH,
+        )
+        copy.start()
+        started.append(copy)
+        return copy
 
     barrier = pltpu.get_barrier_semaphore()
     for k in range(1, ring):
         pl.semaphore_signal(barrier, inc=1, device_id={"row": lax.rem(me + k, ring)}, device_id_type=MESH)
+    for k in range(1, peers):
+        pl.semaphore_signal(barrier, inc=1, device_id={"mol": lax.rem(place + k, peers)}, device_id_type=MESH)
 
     for r in range(local):
         edge_low[r * width : (r + 1) * width, :] = edge_out[:, r * width : (r + 1) * width].astype(BF16)
@@ -124,7 +189,7 @@
     pair_cols[...] = pairs[...].astype(F32).T
 
     def edge_network(m, carry):
-        before = nn(feats[m], low_in) + bias[0:1, :]
+        before = tn(feats[m], low_in) + bias[0:1, :]
         squash = jax.nn.sigmoid(before)
         act = before * squash
         slope[m] = squash + act * (1.0 - squash)
@@ -189,19 +254,7 @@
         return state[layer - 1, rows, :].astype(BF16)
 
     def exchange(stage):
-        copies = []
-        for k in range(1, ring):
-            copy = pltpu.make_async_remote_copy(
-                src_ref=parcels.at[stage, me],
-                dst_ref=parcels.at[stage, me],
-                send_sem=send_sem.at[stage, k - 1],
-                recv_sem=recv_sem.at[stage, k - 1],
-                device_id={"row": lax.rem(me + k, ring)},
-                device_id_type=MESH,
-            )
-            copy.start()
-            copies.append(copy)
-        return copies
+        return [row_copy(stage, k, parcels.at[stage, me], parcels.at[stage, me]) for k in range(1, ring)]
 
     gated_low = [gated[i].astype(BF16) for i in range(2)]
     bias_in = wide(bias, 1, 3)
@@ -209,9 +262,9 @@
     for layer in range(LAYERS):
         parcels[layer, me] = message(layer)
         if layer == 0:
-            pl.semaphore_wait(barrier, ring - 1)
+            pl.semaphore_wait(barrier, ring + peers - 2)
         for copy in exchange(layer):
-            copy.wait()
+            copy.wait_recv()
         joined = jnp.concatenate([parcels[layer, q] for q in range(ring)], axis=1)
         for j in range(ring):
             line, column = iota((ring * WIDE, width), 0), iota((ring * WIDE, width), 1)
@@ -271,7 +324,7 @@
     join = jnp.concatenate([mem_low, read_low], axis=1)
     hidden_low = hidden_w[...].astype(BF16)
     padded[...] = jnp.zeros_like(padded)
-    padded[0:width, 0:n_targets] = final_w[...]
+    padded[0:n_targets, :] = final_w[...]
     final_low = padded[0:width, :].astype(BF16)
     before = nn(join, hidden_low) + bias[11:12, :]
     squash = jax.nn.sigmoid(before)
@@ -280,17 +333,21 @@
     padded[width : width + mols, 0:n_targets] = targets[...]
     padded[width + mols : width + 2 * mols, 0:n_targets] = labels[...].astype(F32)
     label = padded[width + mols : width + 2 * mols, :]
-    gap = nn(inner_low, final_low) + bias[12:13, :] - padded[width : width + mols, :]
+    gap = nt(inner_low, final_low) + bias[12:13, :] - padded[width : width + mols, :]
     loss = jnp.sum(label * gap * gap)
     present = jnp.sum(label)
     spot = iota((8, WIDE), 1)
-    totals[...] = jnp.where(spot == 0, loss, jnp.where(spot == 1, present, 0.0))
+    totals_all[place] = jnp.where(spot == 0, loss, jnp.where(spot == 1, present, 0.0))
+    total_copies = [
+        far_copy(0, k - 1, lax.rem(place + k, peers), totals_all.at[place], totals_all.at[place])
+        for k in range(1, peers)
+    ]
     d_pred = 2.0 * label * gap
     d_pred_low = d_pred.astype(BF16)
-    grad_final[...] = tn(d_pred_low, inner_low)
-    d_before = nt(d_pred_low, final_low) * (squash + inner * (1.0 - squash))
+    head_part[plan.final_at : plan.final_at + 16, :] = tn(d_pred_low, inner_low)[0:16].astype(BF16)
+    d_before = nn(d_pred_low, final_low) * (squash + inner * (1.0 - squash))
     d_before_low = d_before.astype(BF16)
-    grad_hidden[...] = tn(join, d_before_low)
+    head_part[12 * width : 14 * width, :] = tn(join, d_before_low).astype(BF16)
     grad_bias[...] = jnp.zeros_like(grad_bias)
     grad_bias[11:12, :] = jnp.sum(d_before, axis=0, keepdims=True)
     grad_bias[12:13, :] = jnp.sum(d_pred, axis=0, keepdims=True)
@@ -328,7 +385,16 @@
             d_join = nt(d_z_low, memory_low[...])
             d_mem = d_join[:, :width] + d_join[:, 2 * width :]
             d_read = d_join[:, width : 2 * width]
-    grad_memory[...] = tn(jnp.concatenate(joins, axis=0), jnp.concatenate(d_gates, axis=0))
+    grad_memory = tn(jnp.concatenate(joins, axis=0), jnp.concatenate(d_gates, axis=0)).astype(BF16)
+    for i in range(4):
+        head_part[i * 3 * width : (i + 1) * 3 * width, :] = grad_memory[:, i * width : (i + 1) * width]
+    used = plan.final_at + 16
+    head_part[used:, :] = jnp.zeros((ring * plan.head - used, WIDE), BF16)
+    head_copies = []
+    for k in range(1, peers):
+        peer = lax.rem(place + k, peers)
+        rows = rows16(me * plan.head + peer * plan.head_part, plan.head_part)
+        head_copies.append(far_copy(1, k - 1, peer, head_part.at[rows, :], head_recv.at[k - 1]))
     for i in range(4):
         grad_bias[7 + i : 8 + i, :] = d_bias[:, i * width : (i + 1) * width]
     state_grad[...] = tn(jnp.concatenate(lefts, axis=0), jnp.concatenate(rights, axis=0))
@@ -370,7 +436,7 @@
     pick_t = one_hot(iota((half, width), 1) == me * local + iota((half, width), 0) // GROUP)
     pick_n = one_hot(iota((width, half), 0) == me * local + iota((width, half), 1) // GROUP)
 
-    def message_back(layer, gt):
+    def message_back(layer):
         for g in range(groups):
             wide_grad = jnp.where(same_mol_t, nt(pick_t, pulled[layer, g * span : (g + 1) * span, :]), 0.0).astype(BF16)
 
@@ -386,47 +452,55 @@
 
             lax.fori_loop(0, atoms // 2, atoms_pair, 0)
 
-    def run(gt):
-        for layer in reversed(range(LAYERS)):
-            gated_back(layer)
-            message_back(layer, gt)
-            if layer > 0:
-                back = nn(gt[layer * rows_all : (layer + 1) * rows_all, :], edge_low[...]).astype(BF16)
-                for g in range(groups):
-                    reduce_send[g * span : (g + 1) * span, :] = nn(order_back, back[g * span : (g + 1) * span]).astype(BF16)
-                copies = []
-                for k in range(1, ring):
-                    peer = lax.rem(me + k, ring)
-                    copy = pltpu.make_async_remote_copy(
-                        src_ref=reduce_send.at[pl.ds(pl.multiple_of(peer * block, block), block), :],
-                        dst_ref=reduce_recv.at[k - 1],
-                        send_sem=send_sem.at[LAYERS + 1, k - 1],
-                        recv_sem=recv_sem.at[LAYERS + 1, k - 1],
-                        device_id={"row": peer},
-                        device_id_type=MESH,
-                    )
-                    copy.start()
-                    copies.append(copy)
-                for copy in copies:
-                    copy.wait()
-                total = reduce_send[pl.ds(pl.multiple_of(me * block, block), block), :].astype(F32)
-                for k in range(ring - 1):
-                    total = total + reduce_recv[k].astype(F32)
-                parcels[LAYERS, me] = total.astype(BF16)
-                for copy in exchange(LAYERS):
-                    copy.wait()
-                for j in range(ring):
-                    rows = slice(j * block, (j + 1) * block)
-                    state_grad[rows, :] += parcels[LAYERS, j].astype(F32)
-
-        def out_weights(rp, carry):
-            columns = pl.ds(pl.multiple_of(rp * 2 * width, 2 * width), 2 * width)
-            grad_edge[columns, :] = nn(turned_lows[...], gt[:, columns]).T.astype(BF16)
-            return carry
-
-        lax.fori_loop(0, local // 2, out_weights, 0)
-
-    pl.run_scoped(run, pltpu.VMEM((LAYERS * rows_all, local * width), BF16))
+    edge_copies = []
+    for layer in reversed(range(LAYERS)):
+        gated_back(layer)
+        message_back(layer)
+        if layer > 0:
+            back = nn(gt[layer * rows_all : (layer + 1) * rows_all, :], edge_low[...]).astype(BF16)
+            for g in range(groups):
+                reduce_send[g * span : (g + 1) * span, :] = nn(order_back, back[g * span : (g + 1) * span]).astype(BF16)
+            copies = []
+            for k in range(1, ring):
+                rows = rows16(lax.rem(me + k, ring) * block, block)
+                copies.append(row_copy(LAYERS + 1, k, reduce_send.at[rows, :], reduce_recv.at[k - 1]))
+            for copy in copies:
+                copy.wait_recv()
+            total = reduce_send[pl.ds(pl.multiple_of(me * block, block), block), :].astype(F32)
+            for k in range(ring - 1):
+                total = total + reduce_recv[k].astype(F32)
+            parcels[LAYERS, me] = total.astype(BF16)
+            for copy in exchange(LAYERS):
+                copy.wait_recv()
+            for j in range(ring):
+                rows = slice(j * block, (j + 1) * block)
+                state_grad[rows, :] += parcels[LAYERS, j].astype(F32)
+
+    for copy in head_copies:
+        copy.wait_recv()
+    mine = rows16(me * plan.head + place * plan.head_part, plan.head_part)
+    total = head_part[mine, :].astype(F32)
+    for k in range(peers - 1):
+        total = total + head_recv[k].astype(F32)
+    head_all[mine, :] = total.astype(BF16)
+    head_copies[:] = [
+        far_copy(2, k - 1, lax.rem(place + k, peers), head_all.at[mine, :], head_all.at[mine, :])
+        for k in range(1, peers)
+    ]
+
+    chunk = max(plan.edge_part, 2 * width)
+    chunks, parts = plan.edge // chunk, chunk // plan.edge_part
+    home, seat = lax.div(place, parts), lax.rem(place, parts)
+    for j in [*range(1, chunks), 0]:
+        here = lax.rem(home + j, chunks)
+        for i in range(chunk // (2 * width)):
+            columns = pl.ds(pl.multiple_of(here * chunk + i * 2 * width, 2 * width), 2 * width)
+            edge_part[columns, :] = nn(turned_lows[...], gt[:, columns]).T.astype(BF16)
+        for i in range(1 if j == 0 else 0, parts):
+            peer = here * parts + lax.rem(seat + i, parts)
+            k = lax.rem(peer - place + peers, peers)
+            rows = rows16(peer * plan.edge_part, plan.edge_part)
+            edge_copies.append(far_copy(3, k - 1, peer, edge_part.at[rows, :], edge_recv.at[k - 1]))
 
     for g in range(groups):
         wide_grad = jnp.concatenate(
@@ -456,14 +530,90 @@
         column = jnp.sum(jnp.where(lane_mol == m, pair_cols[...], 0.0), axis=1, keepdims=True)
         d_act = nn(one_hot(lane_pair == column), pair_grad[m])
         d_first = d_act * slope[m]
-        total_in = total_in + tn(feats[m], d_first.astype(BF16))
+        total_in = total_in + nn(feats[m], d_first.astype(BF16))
         return (total_in, total_bias + jnp.sum(d_first, axis=0, keepdims=True))
 
     total_in, total_bias = lax.fori_loop(
         0, mols, edge_back, (jnp.zeros((features, width), F32), jnp.zeros((1, width), F32))
     )
-    grad_in[...] = total_in
-    grad_bias[0:1, :] = total_bias
+
+    for s in range(2):
+        for i in range(3):
+            at = (s * 3 + i) * width
+            rest_full[at : at + width, :] = grad_gated[s, :, i * width : (i + 1) * width].astype(BF16)
+    rest_full[plan.bias_at : plan.bias_at + 16, :] = grad_bias[...].astype(BF16)
+    used = plan.bias_at + 16
+    if ring * plan.rest_own > used:
+        rest_full[used:, :] = jnp.zeros((ring * plan.rest_own - used, WIDE), BF16)
+    rest_part[0 : plan.rest_own, :] = rest_full[rows16(me * plan.rest_own, plan.rest_own), :]
+    at = plan.rest_own
+    rest_part[at : at + features, :] = total_in.astype(BF16)
+    at += features
+    rest_part[at : at + 16, :] = jnp.where(iota((16, WIDE), 0) == 0, total_bias, 0.0).astype(BF16)
+    at += 16
+    if plan.rest > at:
+        rest_part[at:, :] = jnp.zeros((plan.rest - at, WIDE), BF16)
+    rest_copies = []
+    for k in range(1, peers):
+        peer = lax.rem(place + k, peers)
+        rows = rows16(peer * plan.rest_part, plan.rest_part)
+        rest_copies.append(far_copy(4, k - 1, peer, rest_part.at[rows, :], rest_recv.at[k - 1]))
+
+    for copy in edge_copies:
+        copy.wait_recv()
+    mine = rows16(place * plan.edge_part, plan.edge_part)
+    total = edge_part[mine, :].astype(F32)
+    for k in range(peers - 1):
+        total = total + edge_recv[k].astype(F32)
+    edge_all[mine, :] = total.astype(BF16)
+    pairs_of = peers // 2
+    line, side = lax.div(place, 2), lax.rem(place, 2)
+    neighbour = line * 2 + 1 - side
+    across = [
+        far_copy(5, k, lax.rem(line + k, pairs_of) * 2 + side, edge_all.at[mine, :], edge_all.at[mine, :])
+        for k in range(1, pairs_of)
+    ]
+    beside = [far_copy(5, 0, neighbour, edge_all.at[mine, :], edge_all.at[mine, :])]
+
+    for copy in head_copies:
+        copy.wait_recv()
+    rows = rows16(me * plan.head, plan.head)
+    head_rows = [row_copy(LAYERS + 2, k, head_all.at[rows, :], head_all.at[rows, :]) for k in range(1, ring)]
+
+    for copy in rest_copies:
+        copy.wait_recv()
+    mine = rows16(place * plan.rest_part, plan.rest_part)
+    total = rest_part[mine, :].astype(F32)
+    for k in range(peers - 1):
+        total = total + rest_recv[k].astype(F32)
+    rest_all[me, mine, :] = total.astype(BF16)
+    rest_copies = [
+        far_copy(6, k - 1, lax.rem(place + k, peers), rest_all.at[me, mine, :], rest_all.at[me, mine, :])
+        for k in range(1, peers)
+    ]
+
+    for k in range(1, pairs_of):
+        across[k - 1].wait_recv()
+        rows = rows16((lax.rem(line - k + pairs_of, pairs_of) * 2 + side) * plan.edge_part, plan.edge_part)
+        beside.append(far_copy(5, pairs_of + k - 1, neighbour, edge_all.at[rows, :], edge_all.at[rows, :]))
+    for copy in rest_copies:
+        copy.wait_recv()
+    rest_rows = [row_copy(LAYERS + 3, k, rest_all.at[me], rest_all.at[me]) for k in range(1, ring)]
+    for copy in total_copies + head_rows:
+        copy.wait_recv()
+    total = totals_all[0]
+    for k in range(1, peers):
+        total = total + totals_all[k]
+    totals[...] = total
+    head_sum[...] = head_all[...]
+    for copy in beside:
+        copy.wait_recv()
+    edge_sum[...] = edge_all[...]
+    for copy in rest_rows:
+        copy.wait_recv()
+    rest_sum[...] = rest_all[...]
+    for copy in started:
+        copy.wait_send()
 
 
 def adamw(weight, first, second, grad, rate):
@@ -473,6 +623,42 @@
     scaled = jnp.sqrt(second_new / (1.0 - BETA_TWO**STEP))
     weight_new = weight - rate * (corrected / (scaled + EPSILON) + DECAY * weight)
     return (weight_new, first_new, second_new, weight_new.astype(BF16))
+
+
+def update_kernel(ring, peers, local, counted, totals, edge_sum, head_sum, rest_sum, *refs):
+    olds, news = refs[:21], refs[23:]
+    loss_out, count_out = refs[21:23]
+    features, width = olds[0].shape
+    plan = Plan(ring, peers, width, local, features)
+    inverse = (1.0 / totals[0:1, :])[0:1, 1:2]
+
+    def update(index, view, grad):
+        parts = [ref[view] for ref in olds[3 * index : 3 * index + 3]]
+        for ref, value in zip(news[4 * index : 4 * index + 4], adamw(*parts, grad * inverse, RATES[index])):
+            ref[view] = value
+
+    for i in range(edge_sum.shape[0] // width):
+        update(1, (slice(None), slice(i * width, (i + 1) * width)), edge_sum[i * width : (i + 1) * width, :].astype(F32))
+
+    @pl.when(pl.program_id(0) == 0)
+    def _():
+        loss_out[0] = counted[0, 0]
+        count_out[0] = counted[0, 1]
+        rest = jnp.concatenate([rest_sum[q, 0 : plan.rest_own, :] for q in range(ring)], axis=0).astype(F32)
+        own = sum(rest_sum[q, plan.rest_own : plan.rest_own + features + 16, :].astype(F32) for q in range(ring))
+        update(0, (slice(None), slice(None)), own[0:features])
+        for s in range(2):
+            for i in range(3):
+                at = (s * 3 + i) * width
+                update(2, (s, slice(None), slice(i * width, (i + 1) * width)), rest[at : at + width])
+        for i in range(4):
+            part = head_sum[i * 3 * width : (i + 1) * 3 * width, :].astype(F32)
+            update(3, (slice(None), slice(i * width, (i + 1) * width)), part)
+        update(4, (slice(None), slice(None)), head_sum[12 * width : 14 * width, :].astype(F32))
+        n_targets = olds[15].shape[0]
+        update(5, (slice(None), slice(None)), head_sum[plan.final_at : plan.final_at + 16, :].astype(F32)[0:n_targets])
+        biases = rest[plan.bias_at : plan.bias_at + 16]
+        update(6, (slice(None), slice(None)), jnp.where(iota((16, WIDE), 0) == 0, own[features : features + 1], biases))
 
 
 def shards(
@@ -514,24 +700,27 @@
     block = rows_all // ring
     n_bias = bias_vector.shape[0]
     n_targets = targets.shape[1]
-    bias_rows = jnp.pad(bias_vector, (0, 16 * WIDE - n_bias)).reshape(16, WIDE)
+    peers = lax.axis_size("mol")
+    plan = Plan(ring, peers, width, local, features)
+
+    def bias_rows(value):
+        return jnp.pad(value, (0, 16 * WIDE - n_bias)).reshape(16, WIDE)
+
+    bias_olds = [bias_rows(value) for value in (bias_vector, bias_first, bias_second)]
+    finals = [value.T for value in (readout_final, readout_final_first, readout_final_second)]
     vmem = pl.BlockSpec(memory_space=pltpu.VMEM)
     smem = pl.BlockSpec(memory_space=pltpu.SMEM)
     shape = jax.ShapeDtypeStruct
-    grad_edge, grad_in, grad_gated, grad_memory, grad_hidden, grad_final, grad_bias, totals = pl.pallas_call(
-        functools.partial(step_kernel, ring),
+    edge_sum, head_sum, rest_sum, totals = pl.pallas_call(
+        functools.partial(step_kernel, ring, peers),
         out_shape=[
-            shape((local * width, width), BF16),
-            shape((features, width), F32),
-            shape((2, width, 3 * width), F32),
-            shape((3 * width, 4 * width), F32),
-            shape((2 * width, width), F32),
-            shape((WIDE, width), F32),
-            shape((16, WIDE), F32),
+            shape((plan.edge, WIDE), BF16),
+            shape((ring * plan.head, WIDE), BF16),
+            shape((ring, plan.rest, WIDE), BF16),
             shape((8, WIDE), F32),
         ],
         in_specs=[smem, smem] + [vmem] * 13,
-        out_specs=[vmem] * 8,
+        out_specs=[vmem] * 4,
         scratch_shapes=[
             pltpu.VMEM((local * width, width), BF16),
             pltpu.VMEM((mols, edges), jnp.int32),
@@ -553,8 +742,24 @@
             pltpu.VMEM((LAYERS + 1, ring, block, WIDE), BF16),
             pltpu.VMEM((rows_all, width), BF16),
             pltpu.VMEM((ring - 1, block, width), BF16),
-            pltpu.SemaphoreType.DMA((LAYERS + 2, ring - 1)),
-            pltpu.SemaphoreType.DMA((LAYERS + 2, ring - 1)),
+            pltpu.VMEM((2, width, 3 * width), F32),
+            pltpu.VMEM((16, WIDE), F32),
+            pltpu.VMEM((peers, 8, WIDE), F32),
+            pltpu.VMEM((plan.edge, WIDE), BF16),
+            pltpu.VMEM((peers - 1, plan.edge_part, WIDE), BF16),
+            pltpu.VMEM((plan.edge, WIDE), BF16),
+            pltpu.VMEM((ring * plan.head, WIDE), BF16),
+            pltpu.VMEM((peers - 1, plan.head_part, WIDE), BF16),
+            pltpu.VMEM((ring * plan.head, WIDE), BF16),
+            pltpu.VMEM((ring * plan.rest_own, WIDE), BF16),
+            pltpu.VMEM((plan.rest, WIDE), BF16),
+            pltpu.VMEM((peers - 1, plan.rest_part, WIDE), BF16),
+            pltpu.VMEM((ring, plan.rest, WIDE), BF16),
+            pltpu.SemaphoreType.DMA((LAYERS + 4, ring - 1)),
+            pltpu.SemaphoreType.DMA((LAYERS + 4, ring - 1)),
+            pltpu.SemaphoreType.DMA((7, peers)),
+            pltpu.SemaphoreType.DMA((7, peers)),
+            pltpu.VMEM((LAYERS * rows_all, local * width), BF16),
         ],
         compiler_params=pltpu.CompilerParams(
             collective_id=0, has_side_effects=True, vmem_limit_bytes=60 * 1024 * 1024
@@ -562,7 +767,7 @@
     )(
         atom_counts,
         edge_counts,
-        edge_feats,
+        jnp.swapaxes(edge_feats, 1, 2),
         edge_source,
         edge_target,
         atom_states.reshape(rows_all, width),
@@ -573,49 +778,39 @@
         gated_weights,
         memory_weights,
         readout_hidden,
-        readout_final,
-        bias_rows,
+        finals[0],
+        bias_olds[0],
     )
-    share = 1.0 / ring
-    spread = jnp.where(jnp.arange(16)[:, None] == 0, 1.0, share)
-    totals = lax.psum(totals, "mol")
-    loss_sum, label_count = totals[0, 0], totals[0, 1]
-    scale = 1.0 / label_count
-    grad_in, grad_gated, grad_memory, grad_hidden, grad_final, grad_bias = lax.psum(
-        (
-            grad_in,
-            grad_gated * share,
-            grad_memory * share,
-            grad_hidden * share,
-            grad_final * share,
-            grad_bias * spread,
-        ),
-        ("mol", "row"),
-    )
-    grad_edge = lax.psum(grad_edge.astype(F32), "mol").reshape(local, width, width)
-    grad_edge = grad_edge.transpose(1, 0, 2).reshape(width, local * width)
-    grads = (
-        grad_in,
-        grad_edge,
-        grad_gated,
-        grad_memory,
-        grad_hidden,
-        grad_final.T[:, :n_targets],
-        grad_bias.reshape(-1)[:n_bias],
-    )
-    kept = (
-        (edge_input, edge_input_first, edge_input_second),
-        (edge_output, edge_output_first, edge_output_second),
-        (gated_weights, gated_first, gated_second),
-        (memory_weights, memory_first, memory_second),
-        (readout_hidden, readout_hidden_first, readout_hidden_second),
-        (readout_final, readout_final_first, readout_final_second),
-        (bias_vector, bias_first, bias_second),
-    )
-    outs = (loss_sum, label_count)
-    for (weight, first, second), grad, rate in zip(kept, grads, RATES):
-        outs += adamw(weight, first, second, grad * scale, rate)
-    return outs
+    olds = [edge_input, edge_input_first, edge_input_second, edge_output, edge_output_first, edge_output_second]
+    olds += [gated_weights, gated_first, gated_second, memory_weights, memory_first, memory_second]
+    olds += [readout_hidden, readout_hidden_first, readout_hidden_second] + finals + bias_olds
+    steps = 8
+    columns = plan.edge // steps
+
+    def whole(value):
+        return pl.BlockSpec(value.shape, lambda i: (0,) * len(value.shape))
+
+    cut = pl.BlockSpec((width, columns), lambda i: (0, i))
+    out_shapes, out_specs = [shape((1,), F32)] * 2, [smem] * 2
+    for index in range(7):
+        old = olds[3 * index]
+        for kind in (F32, F32, F32, BF16):
+            out_shapes.append(shape(old.shape, kind))
+            out_specs.append(cut if index == 1 else whole(old))
+    outs = pl.pallas_call(
+        functools.partial(update_kernel, ring, peers, local),
+        grid=(steps,),
+        out_shape=out_shapes,
+        in_specs=[smem, whole(totals), pl.BlockSpec((columns, WIDE), lambda i: (i, 0)), whole(head_sum), whole(rest_sum)]
+        + [cut if i // 3 == 1 else whole(old) for i, old in enumerate(olds)],
+        out_specs=out_specs,
+        compiler_params=pltpu.CompilerParams(vmem_limit_bytes=60 * 1024 * 1024),
+    )(totals, totals, edge_sum, head_sum, rest_sum, *olds)
+    outs = list(outs)
+    outs[0], outs[1] = outs[0].reshape(()), outs[1].reshape(())
+    outs[22:26] = [value.T for value in outs[22:26]]
+    outs[26:30] = [value.reshape(-1)[:n_bias] for value in outs[26:30]]
+    return tuple(outs)
 
 
 def solution(mesh):

time: 272 us -> 136 us (0.50)
  blocking collectives: 140 us -> 0 us
  Pallas kernels: 87.1 us -> 132 us
  other arithmetic: 21.9 us -> 0 us
  between operations: 14.9 us -> 0.84 us
  local copies, waits for them, and re-layouts: 6.74 us -> 2.62 us
    psum x2 -> x0, blocking collectives: 140 us -> none  [the longest x1 97.8 us: shards(): totals = lax.psum(totals, 'mol')]
    pallas_call x1 -> x2, Pallas kernels: 87.1 us -> 132 us  [the longest x1 118 us: shards(): pl.pallas_call(functools.partial(step_kernel, ring, peers), out_shape=[sh...]
    convert_element_type x7 -> x0, other arithmetic: 14.6 us -> none  [adamw(): return (weight_new, first_new, second_new, weight_new.astype(BF16))]
    mul x4 -> x0, other arithmetic: 6.53 us -> none  [the longest x1 2.08 us: shards(): grad_memory * share]
    unnamed x44 -> x0, local copies, waits for them, and re-layouts: 4.86 us -> none
  transfers between devices with their start and end apart: 1 -> 0, of which waited for: 0 -> 0; matrix products, arithmetic and copies ran while one was open for 3% -> 0% of each run, Pallas kernels for 0% -> 0%
where the time goes in v2:
time: 136 us; the launch traced here: 135 us
  Pallas kernels  132 us (97%)
  local copies, waits for them, and re-layouts  2.62 us (2%)
    pallas_call x1, Pallas kernels, shards(): pl.pallas_call(functools.partial(step_kernel, ring, peers), out_shape=[sh...  118 us
    pallas_call x1, Pallas kernels, shards(): pl.pallas_call(functools.partial(update_kernel, ring, peers, local), grid...  13.5 us

profile of v2, /device:TPU:0, one launch (start us, length us, event | category | flops | bytes accessed | tf_op | source)
XLA Modules:
  0.0 135.2 jit_solution(17861896103426745272)
XLA Ops:
  0.7 1.3 pad_bitcast_fusion.2.bias.refs_18_
  2.0 1.3 pad_bitcast_fusion
  3.3 118.2 %shard_map.508 = (bf16[4096,128]{1,0:T(8,128)(2,1)}, bf16[2048,128]{1,0:T(8,128)(2,1)}, bf16[4,256,128]{2,1,0:T(8,128)(2,1)}, f32[8,128]{1,0:T(8,128)}) custom-call(s32[16]{0:T(128)} %atom_counts.1, s32[16]{0:T(128)} %edge_counts.1, bf16[16,16,384]{2,1,0:T(8,128)(2,1)} %bitcast.25, s32[16,384]{1,0:T(8,128)} %source.1, s32[16,384]{1,0:T(8,128)} %target.1, ...), custom_call_target="tpu_custom_call" | custom-call | tf_op jit(solution)/shard_map/pallas_call | solution.py:714
  121.5 13.5 %shard_map.509 = (f32[1]{0:T(128)}, f32[1]{0:T(128)}, f32[16,128]{1,0:T(8,128)}, f32[16,128]{1,0:T(8,128)}, f32[16,128]{1,0:T(8,128)}, /*index=5*/bf16[16,128]{1...) custom-call(f32[8,128]{1,0:T(8,128)} %get-tuple-element.64.counted.t, ...), custom_call_target="tpu_custom_call" | custom-call | tf_op jit(solution)/shard_map/pallas_call | solution.py:800

commit v3 on v2

--- a/solution.py
+++ b/solution.py
@@ -44,7 +44,7 @@
 
 
 def wide(bias_ref, first, count):
-    return jnp.concatenate([bias_ref[first + i : first + i + 1, :] for i in range(count)], axis=1)
+    return bias_ref[pl.ds(first * WIDE, count * WIDE)].reshape(1, count * WIDE)
 
 
 def round_up(value, unit):
@@ -52,7 +52,7 @@
 
 
 class Plan:
-    def __init__(self, ring, peers, width, local, features):
+    def __init__(self, ring, peers, width, local):
         unit = 16 * peers
         self.edge = local * width
         self.edge_part = self.edge // peers
@@ -61,7 +61,7 @@
         self.head_part = self.head // peers
         self.bias_at = 6 * width
         self.rest_own = round_up(-(-(self.bias_at + 16) // ring), 16)
-        self.rest = round_up(self.rest_own + features + 16, unit)
+        self.rest = round_up(self.rest_own, unit)
         self.rest_part = self.rest // peers
 
 
@@ -77,12 +77,12 @@
     targets,
     labels,
     edge_in,
-    edge_out,
-    gated,
-    memory,
-    hidden_w,
     final_w,
     bias,
+    edge_far,
+    gated_far,
+    memory_far,
+    hidden_far,
     edge_sum,
     head_sum,
     rest_sum,
@@ -125,6 +125,16 @@
     far_send,
     far_recv,
     gt,
+    edge_out,
+    gated,
+    memory,
+    hidden_w,
+    fetch_sem,
+    store_sem,
+    near_recv,
+    near_sum,
+    first_row,
+    first_mol,
 ):
     mols, features, edges = feats.shape
     rows_all, width = states.shape
@@ -137,8 +147,16 @@
     n_targets = targets.shape[1]
     me = lax.axis_index("row")
     place = lax.axis_index("mol")
-    plan = Plan(ring, peers, width, local, features)
+    plan = Plan(ring, peers, width, local)
     started = []
+    fetches = [
+        pltpu.make_async_copy(far, near, fetch_sem.at[i])
+        for i, (far, near) in enumerate(
+            ((edge_far, edge_out), (gated_far, gated), (memory_far, memory), (hidden_far, hidden_w))
+        )
+    ]
+    for copy in fetches:
+        copy.start()
 
     def rows16(start, count):
         return pl.ds(pl.multiple_of(start, 16), count)
@@ -175,10 +193,7 @@
     for k in range(1, peers):
         pl.semaphore_signal(barrier, inc=1, device_id={"mol": lax.rem(place + k, peers)}, device_id_type=MESH)
 
-    for r in range(local):
-        edge_low[r * width : (r + 1) * width, :] = edge_out[:, r * width : (r + 1) * width].astype(BF16)
     low_in = edge_in[...].astype(BF16)
-    memory_low[...] = memory[...].astype(BF16)
 
     lane_edge = iota((1, edges), 1)
     row_index = iota((256, edges), 0)
@@ -188,8 +203,10 @@
         )
     pair_cols[...] = pairs[...].astype(F32).T
 
+    bias_first = wide(bias, 0, 1)
+
     def edge_network(m, carry):
-        before = tn(feats[m], low_in) + bias[0:1, :]
+        before = tn(feats[m], low_in) + bias_first
         squash = jax.nn.sigmoid(before)
         act = before * squash
         slope[m] = squash + act * (1.0 - squash)
@@ -203,7 +220,7 @@
                 sent[rows, a * width : (a + 1) * width] = sums[j * atoms : (j + 1) * atoms]
         return carry
 
-    lax.fori_loop(0, mols, edge_network, 0)
+    lax.fori_loop(0, mols, edge_network, 0, unroll=4)
 
     order = one_hot(
         (iota((span, span), 1) // atoms == iota((span, span), 0) % GROUP)
@@ -235,7 +252,7 @@
                     turned[where, a * width : (a + 1) * width] = tile.astype(BF16)
             return carry
 
-        lax.fori_loop(0, local // 2, rows_pair, 0)
+        lax.fori_loop(0, local // 2, rows_pair, 0, unroll=8)
         packed = jnp.zeros((block, WIDE), F32)
         for g in range(groups):
             base = (g * LAYERS + layer) * half
@@ -256,6 +273,11 @@
     def exchange(stage):
         return [row_copy(stage, k, parcels.at[stage, me], parcels.at[stage, me]) for k in range(1, ring)]
 
+    for copy in fetches:
+        copy.wait()
+    memory_low[...] = memory[...].astype(BF16)
+    for r in range(local):
+        edge_low[r * width : (r + 1) * width, :] = edge_out[:, r * width : (r + 1) * width].astype(BF16)
     gated_low = [gated[i].astype(BF16) for i in range(2)]
     bias_in = wide(bias, 1, 3)
     bias_hid = wide(bias, 4, 3)
@@ -317,23 +339,26 @@
         mem_low = (o * squashed).astype(BF16)
         scores = jnp.where(own, nt(mem_low, atom_low), -1000000000.0)
         weights = jnp.exp(scores - jnp.max(scores, axis=1, keepdims=True))
-        weights = weights / jnp.sum(weights, axis=1, keepdims=True)
+        inverse = 1.0 / jnp.sum(weights, axis=1, keepdims=True)
+        read_low = (nn(weights.astype(BF16), atom_low) * inverse).astype(BF16)
+        weights = weights * inverse
         weights_low = weights.astype(BF16)
-        read_low = nn(weights_low, atom_low).astype(BF16)
         kept.append((join, i, f, c, o, before_cell, squashed, mem_low, weights, weights_low))
     join = jnp.concatenate([mem_low, read_low], axis=1)
     hidden_low = hidden_w[...].astype(BF16)
     padded[...] = jnp.zeros_like(padded)
     padded[0:n_targets, :] = final_w[...]
-    final_low = padded[0:width, :].astype(BF16)
-    before = nn(join, hidden_low) + bias[11:12, :]
+    padded[16:17, 0:n_targets] = bias[pl.ds(12 * WIDE, n_targets)].reshape(1, n_targets)
+    bias_final = padded[16:17, :]
+    final_low = jnp.where(iota((width, WIDE), 0) < n_targets, padded[0:width, :], 0.0).astype(BF16)
+    before = nn(join, hidden_low) + wide(bias, 11, 1)
     squash = jax.nn.sigmoid(before)
     inner = before * squash
     inner_low = inner.astype(BF16)
     padded[width : width + mols, 0:n_targets] = targets[...]
     padded[width + mols : width + 2 * mols, 0:n_targets] = labels[...].astype(F32)
     label = padded[width + mols : width + 2 * mols, :]
-    gap = nt(inner_low, final_low) + bias[12:13, :] - padded[width : width + mols, :]
+    gap = nt(inner_low, final_low) + bias_final - padded[width : width + mols, :]
     loss = jnp.sum(label * gap * gap)
     present = jnp.sum(label)
     spot = iota((8, WIDE), 1)
@@ -415,23 +440,25 @@
             bias_parts[0] = bias_parts[0] + jnp.sum(d_in, axis=0, keepdims=True)
             bias_parts[1] = bias_parts[1] + jnp.sum(d_hid, axis=0, keepdims=True)
             d_in_low, d_hid_low = d_in.astype(BF16), d_hid.astype(BF16)
-            gate_grad[0, rows, :] = d_in_low
-            gate_grad[1, rows, :] = d_hid_low
+            gate_grad[layer, 0, rows, :] = d_in_low
+            gate_grad[layer, 1, rows, :] = d_hid_low
             pulled[layer, rows, :] = nt(d_in_low, gated_low[0]).astype(BF16)
             if layer > 0:
                 state_grad[rows, :] = grad * update + nt(d_hid_low, gated_low[1])
+        for s in range(2):
+            for i in range(3):
+                at = 1 + 3 * s + i
+                grad_bias[at : at + 1, :] += bias_parts[s][:, i * width : (i + 1) * width]
+
+    def gated_weights_back(layer):
         low = states[...] if layer == 0 else state[layer - 1].astype(BF16)
-        d_first = tn(gathered[layer], gate_grad[0])
-        d_second = tn(low, gate_grad[1])
+        d_first = tn(gathered[layer], gate_grad[layer, 0])
+        d_second = tn(low, gate_grad[layer, 1])
         if layer == LAYERS - 1:
             grad_gated[0], grad_gated[1] = d_first, d_second
         else:
             grad_gated[0] += d_first
             grad_gated[1] += d_second
-        for s in range(2):
-            for i in range(3):
-                at = 1 + 3 * s + i
-                grad_bias[at : at + 1, :] += bias_parts[s][:, i * width : (i + 1) * width]
 
     pick_t = one_hot(iota((half, width), 1) == me * local + iota((half, width), 0) // GROUP)
     pick_n = one_hot(iota((width, half), 0) == me * local + iota((width, half), 1) // GROUP)
@@ -450,11 +477,28 @@
                     gt[where, r * width : (r + 1) * width] = tile.astype(BF16)
                 return carry
 
-            lax.fori_loop(0, atoms // 2, atoms_pair, 0)
-
-    edge_copies = []
+            lax.fori_loop(0, atoms // 2, atoms_pair, 0, unroll=8)
+
+    rest_copies = []
     for layer in reversed(range(LAYERS)):
         gated_back(layer)
+        if layer == 0:
+            gated_weights_back(layer)
+            for s in range(2):
+                for i in range(3):
+                    at = (s * 3 + i) * width
+                    rest_full[at : at + width, :] = grad_gated[s, :, i * width : (i + 1) * width].astype(BF16)
+            rest_full[plan.bias_at : plan.bias_at + 16, :] = grad_bias[...].astype(BF16)
+            used = plan.bias_at + 16
+            if ring * plan.rest_own > used:
+                rest_full[used:, :] = jnp.zeros((ring * plan.rest_own - used, WIDE), BF16)
+            rest_part[0 : plan.rest_own, :] = rest_full[rows16(me * plan.rest_own, plan.rest_own), :]
+            if plan.rest > plan.rest_own:
+                rest_part[plan.rest_own :, :] = jnp.zeros((plan.rest - plan.rest_own, WIDE), BF16)
+            for k in range(1, peers):
+                peer = lax.rem(place + k, peers)
+                rows = rows16(peer * plan.rest_part, plan.rest_part)
+                rest_copies.append(far_copy(4, k - 1, peer, rest_part.at[rows, :], rest_recv.at[k - 1]))
         message_back(layer)
         if layer > 0:
             back = nn(gt[layer * rows_all : (layer + 1) * rows_all, :], edge_low[...]).astype(BF16)
@@ -464,6 +508,7 @@
             for k in range(1, ring):
                 rows = rows16(lax.rem(me + k, ring) * block, block)
                 copies.append(row_copy(LAYERS + 1, k, reduce_send.at[rows, :], reduce_recv.at[k - 1]))
+            gated_weights_back(layer)
             for copy in copies:
                 copy.wait_recv()
             total = reduce_send[pl.ds(pl.multiple_of(me * block, block), block), :].astype(F32)
@@ -488,21 +533,57 @@
         for k in range(1, peers)
     ]
 
-    chunk = max(plan.edge_part, 2 * width)
-    chunks, parts = plan.edge // chunk, chunk // plan.edge_part
-    home, seat = lax.div(place, parts), lax.rem(place, parts)
-    for j in [*range(1, chunks), 0]:
-        here = lax.rem(home + j, chunks)
-        for i in range(chunk // (2 * width)):
-            columns = pl.ds(pl.multiple_of(here * chunk + i * 2 * width, 2 * width), 2 * width)
-            edge_part[columns, :] = nn(turned_lows[...], gt[:, columns]).T.astype(BF16)
-        for i in range(1 if j == 0 else 0, parts):
-            peer = here * parts + lax.rem(seat + i, parts)
-            k = lax.rem(peer - place + peers, peers)
-            rows = rows16(peer * plan.edge_part, plan.edge_part)
-            edge_copies.append(far_copy(3, k - 1, peer, edge_part.at[rows, :], edge_recv.at[k - 1]))
-
-    for g in range(groups):
+    lines = peers // 2
+    line, side = lax.div(place, 2), lax.rem(place, 2)
+    neighbour = line * 2 + 1 - side
+    part = plan.edge_part
+    stack = max(1, 2 * width // (2 * part))
+    blocks = lines // stack
+    home, seat = lax.div(line, stack), lax.rem(line, stack)
+
+    def out_weights(start):
+        columns = pl.ds(pl.multiple_of(start, 2 * width), 2 * width)
+        edge_part[columns, :] = nn(turned_lows[...], gt[:, columns]).T.astype(BF16)
+
+    def lines_of(j):
+        return [lax.rem(home + j, blocks) * stack + lax.rem(seat + i, stack) for i in range(stack)]
+
+    def scatter_near(j):
+        copies = []
+        if stack > 1:
+            out_weights(lax.rem(home + j, blocks) * stack * 2 * part)
+        for i, other in enumerate(lines_of(j)):
+            if stack == 1:
+                for step in range(part // (2 * width)):
+                    out_weights(other * 2 * part + (1 - side) * part + step * 2 * width)
+            rows = rows16(other * 2 * part + (1 - side) * part, part)
+            copies.append(far_copy(7, j * stack + i, neighbour, edge_part.at[rows, :], near_recv.at[rows16(other * part, part), :]))
+            if stack == 1:
+                for step in range(part // (2 * width)):
+                    out_weights(other * 2 * part + side * part + step * 2 * width)
+        return copies
+
+    edge_copies = []
+
+    def scatter_far(j, copies):
+        for i, other in enumerate(lines_of(j)):
+            copies[i].wait_recv()
+            rows = rows16(other * part, part)
+            total = edge_part[rows16(other * 2 * part + side * part, part), :].astype(F32) + near_recv[rows, :].astype(F32)
+            near_sum[rows, :] = total.astype(BF16)
+            if j > 0 or i > 0:
+                k = j if stack == 1 else lax.rem(other - line + lines, lines)
+                edge_copies.append(far_copy(3, k - 1, other * 2 + side, near_sum.at[rows, :], edge_recv.at[k - 1]))
+
+    order_of = [*range(1, blocks), 0]
+    waiting = None
+    for j in order_of:
+        copies = scatter_near(j)
+        if waiting is not None:
+            scatter_far(*waiting)
+        waiting = (j, copies)
+
+    def pair_grads(g):
         wide_grad = jnp.concatenate(
             [
                 jnp.where(same_mol, nn(pulled[layer, g * span : (g + 1) * span, :], pick_n), 0.0).astype(BF16)
@@ -511,7 +592,7 @@
             axis=1,
         )
 
-        def pair_back(ap, carry, g=g, wide_grad=wide_grad):
+        def pair_back(ap, carry):
             columns = pl.ds(pl.multiple_of(ap * 2 * width, 2 * width), 2 * width)
             x = nn(wide_grad, turned[g * LAYERS * half : (g + 1) * LAYERS * half, columns]).astype(BF16)
             for s in range(2):
@@ -520,66 +601,11 @@
                     pair_grad[g * GROUP + m, where, :] = x[m * atoms : (m + 1) * atoms, s * width : (s + 1) * width]
             return carry
 
-        lax.fori_loop(0, atoms // 2, pair_back, 0)
-
-    lane_pair = iota((edges, atoms * atoms), 1).astype(F32)
-    lane_mol = iota((edges, mols), 1)
-
-    def edge_back(m, carry):
-        total_in, total_bias = carry
-        column = jnp.sum(jnp.where(lane_mol == m, pair_cols[...], 0.0), axis=1, keepdims=True)
-        d_act = nn(one_hot(lane_pair == column), pair_grad[m])
-        d_first = d_act * slope[m]
-        total_in = total_in + nn(feats[m], d_first.astype(BF16))
-        return (total_in, total_bias + jnp.sum(d_first, axis=0, keepdims=True))
-
-    total_in, total_bias = lax.fori_loop(
-        0, mols, edge_back, (jnp.zeros((features, width), F32), jnp.zeros((1, width), F32))
-    )
-
-    for s in range(2):
-        for i in range(3):
-            at = (s * 3 + i) * width
-            rest_full[at : at + width, :] = grad_gated[s, :, i * width : (i + 1) * width].astype(BF16)
-    rest_full[plan.bias_at : plan.bias_at + 16, :] = grad_bias[...].astype(BF16)
-    used = plan.bias_at + 16
-    if ring * plan.rest_own > used:
-        rest_full[used:, :] = jnp.zeros((ring * plan.rest_own - used, WIDE), BF16)
-    rest_part[0 : plan.rest_own, :] = rest_full[rows16(me * plan.rest_own, plan.rest_own), :]
-    at = plan.rest_own
-    rest_part[at : at + features, :] = total_in.astype(BF16)
-    at += features
-    rest_part[at : at + 16, :] = jnp.where(iota((16, WIDE), 0) == 0, total_bias, 0.0).astype(BF16)
-    at += 16
-    if plan.rest > at:
-        rest_part[at:, :] = jnp.zeros((plan.rest - at, WIDE), BF16)
-    rest_copies = []
-    for k in range(1, peers):
-        peer = lax.rem(place + k, peers)
-        rows = rows16(peer * plan.rest_part, plan.rest_part)
-        rest_copies.append(far_copy(4, k - 1, peer, rest_part.at[rows, :], rest_recv.at[k - 1]))
-
-    for copy in edge_copies:
-        copy.wait_recv()
-    mine = rows16(place * plan.edge_part, plan.edge_part)
-    total = edge_part[mine, :].astype(F32)
-    for k in range(peers - 1):
-        total = total + edge_recv[k].astype(F32)
-    edge_all[mine, :] = total.astype(BF16)
-    pairs_of = peers // 2
-    line, side = lax.div(place, 2), lax.rem(place, 2)
-    neighbour = line * 2 + 1 - side
-    across = [
-        far_copy(5, k, lax.rem(line + k, pairs_of) * 2 + side, edge_all.at[mine, :], edge_all.at[mine, :])
-        for k in range(1, pairs_of)
-    ]
-    beside = [far_copy(5, 0, neighbour, edge_all.at[mine, :], edge_all.at[mine, :])]
-
-    for copy in head_copies:
-        copy.wait_recv()
-    rows = rows16(me * plan.head, plan.head)
-    head_rows = [row_copy(LAYERS + 2, k, head_all.at[rows, :], head_all.at[rows, :]) for k in range(1, ring)]
-
+        lax.fori_loop(0, atoms // 2, pair_back, 0, unroll=8)
+
+    for g in range(groups - 1):
+        pair_grads(g)
+    scatter_far(*waiting)
     for copy in rest_copies:
         copy.wait_recv()
     mine = rows16(place * plan.rest_part, plan.rest_part)
@@ -591,74 +617,203 @@
         far_copy(6, k - 1, lax.rem(place + k, peers), rest_all.at[me, mine, :], rest_all.at[me, mine, :])
         for k in range(1, peers)
     ]
-
-    for k in range(1, pairs_of):
-        across[k - 1].wait_recv()
-        rows = rows16((lax.rem(line - k + pairs_of, pairs_of) * 2 + side) * plan.edge_part, plan.edge_part)
-        beside.append(far_copy(5, pairs_of + k - 1, neighbour, edge_all.at[rows, :], edge_all.at[rows, :]))
-    for copy in rest_copies:
+    for copy in head_copies:
         copy.wait_recv()
-    rest_rows = [row_copy(LAYERS + 3, k, rest_all.at[me], rest_all.at[me]) for k in range(1, ring)]
-    for copy in total_copies + head_rows:
+    rows = rows16(me * plan.head, plan.head)
+    head_rows = [row_copy(LAYERS + 2, k, head_all.at[rows, :], head_all.at[rows, :]) for k in range(1, ring)]
+    pair_grads(groups - 1)
+
+    for copy in edge_copies:
         copy.wait_recv()
-    total = totals_all[0]
+    pieces = 2 if part >= WIDE else 1
+    size = part // pieces
+    across, beside = {}, {}
+    for p in range(pieces):
+        own = rows16(line * part + p * size, size)
+        mine = rows16(place * part + p * size, size)
+        total = near_sum[own, :].astype(F32)
+        for k in range(lines - 1):
+            total = total + edge_recv[k, p * size : (p + 1) * size, :].astype(F32)
+        edge_all[mine, :] = total.astype(BF16)
+        for k in range(1, lines):
+            peer = lax.rem(line + k, lines) * 2 + side
+            across[p, k] = far_copy(5, p * peers + k, peer, edge_all.at[mine, :], edge_all.at[mine, :])
+        beside[p, 0] = far_copy(5, p * peers, neighbour, edge_all.at[mine, :], edge_all.at[mine, :])
+
+    def onward(p):
+        for k in range(1, lines):
+            across[p, k].wait_recv()
+            rows = rows16((lax.rem(line - k + lines, lines) * 2 + side) * part + p * size, size)
+            beside[p, k] = far_copy(5, p * peers + lines + k, neighbour, edge_all.at[rows, :], edge_all.at[rows, :])
+
+    lane_pair = iota((edges, atoms * atoms), 1).astype(F32)
+
+    def edge_back(m):
+        d_act = nn(one_hot(lane_pair == pair_cols[:, m : m + 1]), pair_grad[m])
+        d_first = d_act * slope[m]
+        return nn(feats[m], d_first.astype(BF16)), jnp.sum(d_first, axis=0, keepdims=True)
+
+    total_in, total_bias = edge_back(0)
+    for m in range(1, mols):
+        if m == mols // 2:
+            for copy in rest_copies:
+                copy.wait_recv()
+            rest_rows = [row_copy(LAYERS + 3, k, rest_all.at[me], rest_all.at[me]) for k in range(1, ring)]
+        more_in, more_bias = edge_back(m)
+        total_in, total_bias = total_in + more_in, total_bias + more_bias
+    first_row[me, 0:features, :] = total_in
+    first_row[me, features : features + 8, :] = jnp.broadcast_to(total_bias, (8, width))
+    first_copies = [row_copy(LAYERS + 4, k, first_row.at[me], first_row.at[me]) for k in range(1, ring)]
+    onward(0)
+    for copy in first_copies:
+        copy.wait_recv()
+    total = first_row[0]
+    for q in range(1, ring):
+        total = total + first_row[q]
+    first_mol[place] = total
+    first_copies = [
+        far_copy(8, k - 1, lax.rem(place + k, peers), first_mol.at[place], first_mol.at[place])
+        for k in range(1, peers)
+    ]
+    for p in range(1, pieces):
+        onward(p)
+
+    stores = []
+
+    def store(source_ref, target_ref):
+        copy = pltpu.make_async_copy(source_ref, target_ref, store_sem.at[len(stores)])
+        copy.start()
+        stores.append(copy)
+
+    for copy in head_rows:
+        copy.wait_recv()
+    store(head_all, head_sum)
+    for copy in rest_rows:
+        copy.wait_recv()
+    store(rest_all, rest_sum)
+    for copy in total_copies + first_copies:
+        copy.wait_recv()
+    total, total_first = totals_all[0], first_mol[0]
     for k in range(1, peers):
         total = total + totals_all[k]
-    totals[...] = total
-    head_sum[...] = head_all[...]
-    for copy in beside:
+        total_first = total_first + first_mol[k]
+    totals[0:8, :] = total
+    totals[8:, :] = total_first
+    for copy in beside.values():
         copy.wait_recv()
-    edge_sum[...] = edge_all[...]
-    for copy in rest_rows:
-        copy.wait_recv()
-    rest_sum[...] = rest_all[...]
+    store(edge_all, edge_sum)
     for copy in started:
         copy.wait_send()
+    for copy in stores:
+        copy.wait()
 
 
 def adamw(weight, first, second, grad, rate):
     first_new = BETA_ONE * first + (1.0 - BETA_ONE) * grad
     second_new = BETA_TWO * second + (1.0 - BETA_TWO) * grad * grad
-    corrected = first_new / (1.0 - BETA_ONE**STEP)
-    scaled = jnp.sqrt(second_new / (1.0 - BETA_TWO**STEP))
-    weight_new = weight - rate * (corrected / (scaled + EPSILON) + DECAY * weight)
+    scaled = jnp.sqrt(second_new * (1.0 / (1.0 - BETA_TWO**STEP))) + EPSILON
+    weight_new = (1.0 - rate * DECAY) * weight - (rate / (1.0 - BETA_ONE**STEP)) * first_new / scaled
     return (weight_new, first_new, second_new, weight_new.astype(BF16))
 
 
-def update_kernel(ring, peers, local, counted, totals, edge_sum, head_sum, rest_sum, *refs):
-    olds, news = refs[:21], refs[23:]
-    loss_out, count_out = refs[21:23]
+PIECES = 4
+
+
+def update_kernel(ring, peers, local, counted, totals, edge_far, head_far, rest_far, *refs):
+    fars, refs = refs[:21], refs[21:]
+    (loss_out, count_out), refs = refs[:2], refs[2:]
+    outs, refs = refs[:28], refs[28:]
+    (edge_sum, head_sum, rest_sum), refs = refs[:3], refs[3:]
+    olds, refs = refs[:21], refs[21:]
+    news, (fetch_sem, store_sem) = refs[:28], refs[28:]
     features, width = olds[0].shape
-    plan = Plan(ring, peers, width, local, features)
+    n_bias = olds[18].shape[0]
+    plan = Plan(ring, peers, width, local)
+    every = slice(None)
+    columns = plan.edge // PIECES
+    cuts = [(every, pl.ds(i * columns, columns)) for i in range(PIECES)]
+    count = [0, 0]
+
+    def copies_of(sides, sem, which):
+        made = []
+        for source_ref, target_ref in sides:
+            made.append(pltpu.make_async_copy(source_ref, target_ref, sem.at[count[which]]))
+            made[-1].start()
+            count[which] += 1
+        return made
+
+    def fetch(index, cut=None):
+        where = range(3 * index, 3 * index + 3)
+        return copies_of([(fars[i], olds[i]) if cut is None else (fars[i].at[cut], olds[i].at[cut]) for i in where], fetch_sem, 0)
+
+    def store(index, cut=None):
+        where = range(4 * index, 4 * index + 4)
+        return copies_of([(news[i], outs[i]) if cut is None else (news[i].at[cut], outs[i].at[cut]) for i in where], store_sem, 1)
+
+    edge_ready = copies_of([(edge_far, edge_sum)], fetch_sem, 0)
+    cut_ready = [fetch(1, cut) for cut in cuts]
+    head_ready = copies_of([(head_far, head_sum)], fetch_sem, 0)
+    ready = {index: fetch(index) for index in (3, 4, 5)}
+    rest_ready = copies_of([(rest_far, rest_sum)], fetch_sem, 0)
+    ready.update({index: fetch(index) for index in (2, 0, 6)})
+    loss_out[0] = counted[0, 0]
+    count_out[0] = counted[0, 1]
     inverse = (1.0 / totals[0:1, :])[0:1, 1:2]
 
     def update(index, view, grad):
         parts = [ref[view] for ref in olds[3 * index : 3 * index + 3]]
-        for ref, value in zip(news[4 * index : 4 * index + 4], adamw(*parts, grad * inverse, RATES[index])):
+        for ref, value in zip(news[4 * index : 4 * index + 4], adamw(*parts, grad, RATES[index])):
             ref[view] = value
 
-    for i in range(edge_sum.shape[0] // width):
-        update(1, (slice(None), slice(i * width, (i + 1) * width)), edge_sum[i * width : (i + 1) * width, :].astype(F32))
-
-    @pl.when(pl.program_id(0) == 0)
-    def _():
-        loss_out[0] = counted[0, 0]
-        count_out[0] = counted[0, 1]
-        rest = jnp.concatenate([rest_sum[q, 0 : plan.rest_own, :] for q in range(ring)], axis=0).astype(F32)
-        own = sum(rest_sum[q, plan.rest_own : plan.rest_own + features + 16, :].astype(F32) for q in range(ring))
-        update(0, (slice(None), slice(None)), own[0:features])
-        for s in range(2):
-            for i in range(3):
-                at = (s * 3 + i) * width
-                update(2, (s, slice(None), slice(i * width, (i + 1) * width)), rest[at : at + width])
-        for i in range(4):
-            part = head_sum[i * 3 * width : (i + 1) * 3 * width, :].astype(F32)
-            update(3, (slice(None), slice(i * width, (i + 1) * width)), part)
-        update(4, (slice(None), slice(None)), head_sum[12 * width : 14 * width, :].astype(F32))
-        n_targets = olds[15].shape[0]
-        update(5, (slice(None), slice(None)), head_sum[plan.final_at : plan.final_at + 16, :].astype(F32)[0:n_targets])
-        biases = rest[plan.bias_at : plan.bias_at + 16]
-        update(6, (slice(None), slice(None)), jnp.where(iota((16, WIDE), 0) == 0, own[features : features + 1], biases))
+    def wait(copies):
+        for copy in copies:
+            copy.wait()
+
+    stored = []
+    wait(edge_ready)
+    for p in range(PIECES):
+        wait(cut_ready[p])
+        for i in range(p * columns // width, (p + 1) * columns // width):
+            grad = edge_sum[i * width : (i + 1) * width, :].astype(F32) * inverse
+            update(1, (every, slice(i * width, (i + 1) * width)), grad)
+        stored += store(1, cuts[p])
+    wait(head_ready + ready[3])
+    for i in range(4):
+        grad = head_sum[i * 3 * width : (i + 1) * 3 * width, :].astype(F32) * inverse
+        update(3, (every, slice(i * width, (i + 1) * width)), grad)
+    stored += store(3)
+    wait(rest_ready + ready[2])
+    for s in range(2):
+        for i in range(3):
+            at, end = (s * 3 + i) * width, (s * 3 + i + 1) * width
+            while at < end:
+                q, low = divmod(at, plan.rest_own)
+                rows = min(end - at, plan.rest_own - low)
+                first = at - (s * 3 + i) * width
+                grad = rest_sum[q, low : low + rows, :].astype(F32) * inverse
+                update(2, (s, slice(first, first + rows), slice(i * width, (i + 1) * width)), grad)
+                at += rows
+    stored += store(2)
+    wait(ready[4])
+    update(4, (every, every), head_sum[12 * width : 14 * width, :].astype(F32) * inverse)
+    stored += store(4)
+    wait(ready[5])
+    n_targets = olds[15].shape[0]
+    update(5, (every, every), (head_sum[plan.final_at : plan.final_at + 16, :].astype(F32) * inverse)[0:n_targets])
+    stored += store(5)
+    own = totals[8:, :] * inverse
+    wait(ready[0])
+    update(0, (every, every), own[0:features])
+    stored += store(0)
+    q, low = divmod(plan.bias_at, plan.rest_own)
+    biases = rest_sum[q, low : low + 16, :].astype(F32) * inverse
+    wait(ready[6])
+    for i in range(-(-n_bias // WIDE)):
+        size = min(WIDE, n_bias - i * WIDE)
+        grad = (own[features : features + 1] if i == 0 else biases[i : i + 1])[:, 0:size]
+        update(6, pl.ds(i * WIDE, size), grad.reshape(size))
+    stored += store(6)
+    wait(stored)
 
 
 def shards(
@@ -698,18 +853,13 @@
     local = width // ring
     rows_all = mols * atoms
     block = rows_all // ring
-    n_bias = bias_vector.shape[0]
-    n_targets = targets.shape[1]
     peers = lax.axis_size("mol")
-    plan = Plan(ring, peers, width, local, features)
-
-    def bias_rows(value):
-        return jnp.pad(value, (0, 16 * WIDE - n_bias)).reshape(16, WIDE)
-
-    bias_olds = [bias_rows(value) for value in (bias_vector, bias_first, bias_second)]
+    plan = Plan(ring, peers, width, local)
+
     finals = [value.T for value in (readout_final, readout_final_first, readout_final_second)]
     vmem = pl.BlockSpec(memory_space=pltpu.VMEM)
     smem = pl.BlockSpec(memory_space=pltpu.SMEM)
+    far = pl.BlockSpec(memory_space=pl.ANY)
     shape = jax.ShapeDtypeStruct
     edge_sum, head_sum, rest_sum, totals = pl.pallas_call(
         functools.partial(step_kernel, ring, peers),
@@ -717,10 +867,10 @@
             shape((plan.edge, WIDE), BF16),
             shape((ring * plan.head, WIDE), BF16),
             shape((ring, plan.rest, WIDE), BF16),
-            shape((8, WIDE), F32),
+            shape((8 + features + 8, WIDE), F32),
         ],
-        in_specs=[smem, smem] + [vmem] * 13,
-        out_specs=[vmem] * 4,
+        in_specs=[smem, smem] + [vmem] * 9 + [far] * 4,
+        out_specs=[far] * 3 + [vmem],
         scratch_shapes=[
             pltpu.VMEM((local * width, width), BF16),
             pltpu.VMEM((mols, edges), jnp.int32),
@@ -735,7 +885,7 @@
             pltpu.VMEM((LAYERS, 4, rows_all, width), F32),
             pltpu.VMEM((LAYERS, rows_all, width), F32),
             pltpu.VMEM((rows_all, width), F32),
-            pltpu.VMEM((2, rows_all, 3 * width), BF16),
+            pltpu.VMEM((LAYERS, 2, rows_all, 3 * width), BF16),
             pltpu.VMEM((LAYERS, rows_all, width), BF16),
             pltpu.VMEM((3 * width, 4 * width), BF16),
             pltpu.VMEM((width + 2 * mols, WIDE), F32),
@@ -746,7 +896,7 @@
             pltpu.VMEM((16, WIDE), F32),
             pltpu.VMEM((peers, 8, WIDE), F32),
             pltpu.VMEM((plan.edge, WIDE), BF16),
-            pltpu.VMEM((peers - 1, plan.edge_part, WIDE), BF16),
+            pltpu.VMEM((peers // 2 - 1, plan.edge_part, WIDE), BF16),
             pltpu.VMEM((plan.edge, WIDE), BF16),
             pltpu.VMEM((ring * plan.head, WIDE), BF16),
             pltpu.VMEM((peers - 1, plan.head_part, WIDE), BF16),
@@ -755,11 +905,21 @@
             pltpu.VMEM((plan.rest, WIDE), BF16),
             pltpu.VMEM((peers - 1, plan.rest_part, WIDE), BF16),
             pltpu.VMEM((ring, plan.rest, WIDE), BF16),
-            pltpu.SemaphoreType.DMA((LAYERS + 4, ring - 1)),
-            pltpu.SemaphoreType.DMA((LAYERS + 4, ring - 1)),
-            pltpu.SemaphoreType.DMA((7, peers)),
-            pltpu.SemaphoreType.DMA((7, peers)),
+            pltpu.SemaphoreType.DMA((LAYERS + 5, ring - 1)),
+            pltpu.SemaphoreType.DMA((LAYERS + 5, ring - 1)),
+            pltpu.SemaphoreType.DMA((9, 2 * peers)),
+            pltpu.SemaphoreType.DMA((9, 2 * peers)),
             pltpu.VMEM((LAYERS * rows_all, local * width), BF16),
+            pltpu.VMEM(edge_output.shape, F32),
+            pltpu.VMEM(gated_weights.shape, F32),
+            pltpu.VMEM(memory_weights.shape, F32),
+            pltpu.VMEM(readout_hidden.shape, F32),
+            pltpu.SemaphoreType.DMA((4,)),
+            pltpu.SemaphoreType.DMA((3,)),
+            pltpu.VMEM((peers // 2 * plan.edge_part, WIDE), BF16),
+            pltpu.VMEM((peers // 2 * plan.edge_part, WIDE), BF16),
+            pltpu.VMEM((ring, features + 8, WIDE), F32),
+            pltpu.VMEM((peers, features + 8, WIDE), F32),
         ],
         compiler_params=pltpu.CompilerParams(
             collective_id=0, has_side_effects=True, vmem_limit_bytes=60 * 1024 * 1024
@@ -774,42 +934,31 @@
         targets,
         label_mask,
         edge_input,
+        finals[0],
+        bias_vector,
         edge_output,
         gated_weights,
         memory_weights,
         readout_hidden,
-        finals[0],
-        bias_olds[0],
     )
     olds = [edge_input, edge_input_first, edge_input_second, edge_output, edge_output_first, edge_output_second]
     olds += [gated_weights, gated_first, gated_second, memory_weights, memory_first, memory_second]
-    olds += [readout_hidden, readout_hidden_first, readout_hidden_second] + finals + bias_olds
-    steps = 8
-    columns = plan.edge // steps
-
-    def whole(value):
-        return pl.BlockSpec(value.shape, lambda i: (0,) * len(value.shape))
-
-    cut = pl.BlockSpec((width, columns), lambda i: (0, i))
-    out_shapes, out_specs = [shape((1,), F32)] * 2, [smem] * 2
-    for index in range(7):
-        old = olds[3 * index]
-        for kind in (F32, F32, F32, BF16):
-            out_shapes.append(shape(old.shape, kind))
-            out_specs.append(cut if index == 1 else whole(old))
+    olds += [readout_hidden, readout_hidden_first, readout_hidden_second] + finals
+    olds += [bias_vector, bias_first, bias_second]
+    news = [shape(olds[3 * index].shape, kind) for index in range(7) for kind in (F32, F32, F32, BF16)]
+    sums = [edge_sum, head_sum, rest_sum]
     outs = pl.pallas_call(
         functools.partial(update_kernel, ring, peers, local),
-        grid=(steps,),
-        out_shape=out_shapes,
-        in_specs=[smem, whole(totals), pl.BlockSpec((columns, WIDE), lambda i: (i, 0)), whole(head_sum), whole(rest_sum)]
-        + [cut if i // 3 == 1 else whole(old) for i, old in enumerate(olds)],
-        out_specs=out_specs,
+        out_shape=[shape((1,), F32)] * 2 + news,
+        in_specs=[smem, vmem] + [far] * 24,
+        out_specs=[smem] * 2 + [far] * 28,
+        scratch_shapes=[pltpu.VMEM(value.shape, value.dtype) for value in sums + olds + news]
+        + [pltpu.SemaphoreType.DMA((3 + 18 + 3 * PIECES,)), pltpu.SemaphoreType.DMA((24 + 4 * PIECES,))],
         compiler_params=pltpu.CompilerParams(vmem_limit_bytes=60 * 1024 * 1024),
-    )(totals, totals, edge_sum, head_sum, rest_sum, *olds)
+    )(totals, totals, *sums, *olds)
     outs = list(outs)
     outs[0], outs[1] = outs[0].reshape(()), outs[1].reshape(())
     outs[22:26] = [value.T for value in outs[22:26]]
-    outs[26:30] = [value.reshape(-1)[:n_bias] for value in outs[26:30]]
     return tuple(outs)
 
 

time: 136 us -> 104 us (0.76)
  Pallas kernels: 132 us -> 102 us
  local copies, waits for them, and re-layouts: 2.62 us -> 0 us
    pallas_call x1, Pallas kernels: 118 us -> 91 us  [shards(): pl.pallas_call(functools.partial(step_kernel, ring, peers), out_shape=[sh...]
    pallas_call x1, Pallas kernels: 13.5 us -> 10.8 us  [shards(): pl.pallas_call(functools.partial(update_kernel, ring, peers, local), out_...]
    reshape x2 -> x0, local copies, waits for them, and re-layouts: 2.62 us -> none  [bias_rows(): return jnp.pad(value, (0, 16 * WIDE - n_bias)).reshape(16, WIDE)]
where the time goes in v3:
time: 104 us; the launch traced here: 103 us
  Pallas kernels  102 us (98%)
    pallas_call x1, Pallas kernels, shards(): pl.pallas_call(functools.partial(step_kernel, ring, peers), out_shape=[sh...  91 us
    pallas_call x1, Pallas kernels, shards(): pl.pallas_call(functools.partial(update_kernel, ring, peers, local), out_...  10.8 us

profile of v3, /device:TPU:0, one launch (start us, length us, event | category | flops | bytes accessed | tf_op | source)
XLA Modules:
  0.0 102.7 jit_solution(13859792310249544109)
XLA Ops:
  0.7 91.0 %shard_map.508 = (bf16[4096,128]{1,0:T(8,128)(2,1)}, bf16[2048,128]{1,0:T(8,128)(2,1)}, bf16[4,256,128]{2,1,0:T(8,128)(2,1)}, f32[32,128]{1,0:T(8,128)}) custom-call(s32[16]{0:T(128)} %atom_counts.1, s32[16]{0:T(128)} %edge_counts.1, bf16[16,16,384]{2,1,0:T(8,128)(2,1)} %bitcast.11, s32[16,384]{1,0:T(8,128)} %source.1, s32[16,384]{1,0:T(8,128)} %target.1, ...), custom_call_target="tpu_custom_call" | custom-call | tf_op jit(solution)/shard_map/pallas_call | solution.py:864
  91.7 10.8 %shard_map.509 = (f32[1]{0:T(128)}, f32[1]{0:T(128)}, f32[16,128]{1,0:T(8,128)}, f32[16,128]{1,0:T(8,128)}, f32[16,128]{1,0:T(8,128)}, /*index=5*/bf16[16,128]{1...) custom-call(f32[32,128]{1,0:T(8,128)} %get-tuple-element.64.counted., ...), custom_call_target="tpu_custom_call" | custom-call | tf_op jit(solution)/shard_map/pallas_call | solution.py:950

commit v4 on v3

--- a/solution.py
+++ b/solution.py
@@ -63,6 +63,10 @@
         self.rest_own = round_up(-(-(self.bias_at + 16) // ring), 16)
         self.rest = round_up(self.rest_own, unit)
         self.rest_part = self.rest // peers
+        self.pieces = 2 if self.edge_part >= WIDE else 1
+        sizes = [peers - 1] * 9
+        sizes[3], sizes[5], sizes[7] = peers // 2 - 1, self.pieces * peers, peers // 2
+        self.stages = [sum(sizes[:stage]) for stage in range(10)]
 
 
 def step_kernel(
@@ -94,7 +98,6 @@
     turned,
     slope,
     pair_grad,
-    lows,
     turned_lows,
     gathered,
     gates,
@@ -135,6 +138,7 @@
     near_sum,
     first_row,
     first_mol,
+    first_grad,
 ):
     mols, features, edges = feats.shape
     rows_all, width = states.shape
@@ -143,7 +147,7 @@
     groups = mols // GROUP
     span = GROUP * atoms
     half = GROUP * local
-    block = rows_all // ring
+    block = span // ring
     n_targets = targets.shape[1]
     me = lax.axis_index("row")
     place = lax.axis_index("mol")
@@ -162,11 +166,12 @@
         return pl.ds(pl.multiple_of(start, 16), count)
 
     def far_copy(stage, index, peer, source_ref, target_ref):
+        index += plan.stages[stage]
         copy = pltpu.make_async_remote_copy(
             src_ref=source_ref,
             dst_ref=target_ref,
-            send_sem=far_send.at[stage, index],
-            recv_sem=far_recv.at[stage, index],
+            send_sem=far_send.at[index],
+            recv_sem=far_recv.at[index],
             device_id={"mol": peer},
             device_id_type=MESH,
         )
@@ -233,77 +238,56 @@
     same_mol = iota((span, half), 0) // atoms == iota((span, half), 1) % GROUP
     same_mol_t = iota((half, span), 0) % GROUP == iota((half, span), 1) // atoms
 
-    def message(layer):
-        for g in range(groups):
-            lows[layer, g * span : (g + 1) * span, :] = nn(
-                order, state_low(layer, g)
-            ).astype(BF16)
-        low_p = lows[layer]
-        turned_lows[:, layer * rows_all : (layer + 1) * rows_all] = low_p.astype(F32).T.astype(BF16)
-
-        def rows_pair(rp, carry):
-            t = nt(low_p, edge_low[pl.ds(pl.multiple_of(rp * 2 * width, 2 * width), 2 * width), :])
-            for g in range(groups):
-                base = (g * LAYERS + layer) * half
-                where = pl.ds(pl.multiple_of(base + rp * 16, 16), 16)
-                for a in range(atoms):
-                    at = g * span + a * GROUP
-                    tile = jnp.concatenate([t[at : at + GROUP, :width], t[at : at + GROUP, width:]], axis=0)
-                    turned[where, a * width : (a + 1) * width] = tile.astype(BF16)
-            return carry
-
-        lax.fori_loop(0, local // 2, rows_pair, 0, unroll=8)
-        packed = jnp.zeros((block, WIDE), F32)
-        for g in range(groups):
-            base = (g * LAYERS + layer) * half
-            u = nt(sent[g * span : (g + 1) * span, :], turned[base : base + half, :])
-            u = jnp.where(same_mol, u, 0.0).astype(BF16)
-            for j in range(span // block):
-                slot = g * (span // block) + j
-                pick = one_hot(iota((half, WIDE), 1) == slot * local + iota((half, WIDE), 0) // GROUP)
-                packed = packed + nn(u[j * block : (j + 1) * block], pick)
-        return packed.astype(BF16)
-
-    def state_low(layer, g):
-        rows = slice(g * span, (g + 1) * span)
+    def state_low(layer, rows):
         if layer == 0:
             return states[rows, :]
         return state[layer - 1, rows, :].astype(BF16)
 
+    def message(layer, g):
+        rows = slice(g * span, (g + 1) * span)
+        low_p = nn(order, state_low(layer, rows)).astype(BF16)
+        at = layer * rows_all + g * span
+        turned_lows[:, at : at + span] = low_p.astype(F32).T.astype(BF16)
+        base = (g * LAYERS + layer) * half
+
+        def rows_pair(rp, carry):
+            t = nt(low_p, edge_low[pl.ds(pl.multiple_of(rp * 2 * width, 2 * width), 2 * width), :])
+            where = pl.ds(pl.multiple_of(base + rp * 16, 16), 16)
+            for a in range(atoms):
+                at = a * GROUP
+                tile = jnp.concatenate([t[at : at + GROUP, :width], t[at : at + GROUP, width:]], axis=0)
+                turned[where, a * width : (a + 1) * width] = tile.astype(BF16)
+            return carry
+
+        lax.fori_loop(0, local // 2, rows_pair, 0, unroll=8)
+        u = nt(sent[rows, :], turned[base : base + half, :])
+        u = jnp.where(same_mol, u, 0.0).astype(BF16)
+        packed = jnp.zeros((block, WIDE), F32)
+        for j in range(ring):
+            pick = one_hot(iota((half, WIDE), 1) == j * local + iota((half, WIDE), 0) // GROUP)
+            packed = packed + nn(u[j * block : (j + 1) * block], pick)
+        parcels[layer * groups + g, me] = packed.astype(BF16)
+
     def exchange(stage):
         return [row_copy(stage, k, parcels.at[stage, me], parcels.at[stage, me]) for k in range(1, ring)]
 
-    for copy in fetches:
-        copy.wait()
-    memory_low[...] = memory[...].astype(BF16)
-    for r in range(local):
-        edge_low[r * width : (r + 1) * width, :] = edge_out[:, r * width : (r + 1) * width].astype(BF16)
-    gated_low = [gated[i].astype(BF16) for i in range(2)]
-    bias_in = wide(bias, 1, 3)
-    bias_hid = wide(bias, 4, 3)
-    for layer in range(LAYERS):
-        parcels[layer, me] = message(layer)
-        if layer == 0:
-            pl.semaphore_wait(barrier, ring + peers - 2)
-        for copy in exchange(layer):
-            copy.wait_recv()
-        joined = jnp.concatenate([parcels[layer, q] for q in range(ring)], axis=1)
-        for j in range(ring):
-            line, column = iota((ring * WIDE, width), 0), iota((ring * WIDE, width), 1)
-            pick = one_hot(
-                (line % WIDE // local == j) & (line // WIDE == column // local) & (line % local == column % local)
-            )
-            rows = slice(j * block, (j + 1) * block)
-            got = nn(joined, pick).astype(BF16)
+    def gated_step(layer, g):
+        stage = layer * groups + g
+        joined = jnp.concatenate([parcels[stage, q] for q in range(ring)], axis=1)
+        for j in range(0, ring, 2):
+            parts = []
+            for i in (j, j + 1):
+                row, column = iota((ring * WIDE, width), 0), iota((ring * WIDE, width), 1)
+                pick = one_hot(
+                    (row % WIDE // local == i) & (row // WIDE == column // local) & (row % local == column % local)
+                )
+                parts.append(nn(joined, pick))
+            rows = slice(g * span + j * block, g * span + (j + 2) * block)
+            got = jnp.concatenate(parts, axis=0).astype(BF16)
             gathered[layer, rows, :] = got
-            if layer == 0:
-                low = states[rows, :]
-                old = low.astype(F32)
-            else:
-                old = state[layer - 1, rows, :]
-                low = old.astype(BF16)
+            old = states[rows, :].astype(F32) if layer == 0 else state[layer - 1, rows, :]
             gate_in = nn(got, gated_low[0]) + bias_in
-            gate_hid = nn(low, gated_low[1]) + bias_hid
+            gate_hid = nn(state_low(layer, rows), gated_low[1]) + bias_hid
             reset = jax.nn.sigmoid(gate_in[:, :width] + gate_hid[:, :width])
             update = jax.nn.sigmoid(gate_in[:, width : 2 * width] + gate_hid[:, width : 2 * width])
             third = gate_hid[:, 2 * width :]
@@ -313,6 +297,29 @@
             gates[layer, 2, rows, :] = candidate
             gates[layer, 3, rows, :] = third
             state[layer, rows, :] = (1.0 - update) * candidate + update * old
+
+    for copy in fetches:
+        copy.wait()
+    memory_low[...] = memory[...].astype(BF16)
+    for r in range(local):
+        edge_low[r * width : (r + 1) * width, :] = edge_out[:, r * width : (r + 1) * width].astype(BF16)
+    gated_low = [gated[i].astype(BF16) for i in range(2)]
+    bias_in = wide(bias, 1, 3)
+    bias_hid = wide(bias, 4, 3)
+    flying = {}
+    for g in range(groups):
+        message(0, g)
+        if g == 0:
+            pl.semaphore_wait(barrier, ring + peers - 2)
+        flying[0, g] = exchange(g)
+    for layer in range(LAYERS):
+        for g in range(groups):
+            for copy in flying[layer, g]:
+                copy.wait_recv()
+            gated_step(layer, g)
+            if layer + 1 < LAYERS:
+                message(layer + 1, g)
+                flying[layer + 1, g] = exchange((layer + 1) * groups + g)
 
     atom_low = state[LAYERS - 1].astype(BF16)
     counts = jnp.zeros((mols, 1), jnp.int32)
@@ -424,10 +431,10 @@
         grad_bias[7 + i : 8 + i, :] = d_bias[:, i * width : (i + 1) * width]
     state_grad[...] = tn(jnp.concatenate(lefts, axis=0), jnp.concatenate(rights, axis=0))
 
-    def gated_back(layer):
+    def gated_back(layer, g):
         bias_parts = [jnp.zeros((1, 3 * width), F32) for _ in range(2)]
-        for j in range(ring):
-            rows = slice(j * block, (j + 1) * block)
+        for j in range(2):
+            rows = slice(g * span + j * span // 2, g * span + (j + 1) * span // 2)
             reset, update = gates[layer, 0, rows, :], gates[layer, 1, rows, :]
             candidate, third = gates[layer, 2, rows, :], gates[layer, 3, rows, :]
             old = states[rows, :].astype(F32) if layer == 0 else state[layer - 1, rows, :]
@@ -463,27 +470,55 @@
     pick_t = one_hot(iota((half, width), 1) == me * local + iota((half, width), 0) // GROUP)
     pick_n = one_hot(iota((width, half), 0) == me * local + iota((width, half), 1) // GROUP)
 
-    def message_back(layer):
+    def message_back(layer, g):
+        rows = slice(g * span, (g + 1) * span)
+        wide_grad = jnp.where(same_mol_t, nt(pick_t, pulled[layer, rows, :]), 0.0).astype(BF16)
+
+        def atoms_pair(ap, carry):
+            columns = pl.ds(pl.multiple_of(ap * 2 * width, 2 * width), 2 * width)
+            x = nn(wide_grad, sent[rows, columns])
+            where = pl.ds(pl.multiple_of(layer * rows_all + g * span + ap * 16, 16), 16)
+            for r in range(local):
+                at = r * GROUP
+                tile = jnp.concatenate([x[at : at + GROUP, :width], x[at : at + GROUP, width:]], axis=0)
+                gt[where, r * width : (r + 1) * width] = tile.astype(BF16)
+            return carry
+
+        lax.fori_loop(0, atoms // 2, atoms_pair, 0, unroll=8)
+
+    last = LAYERS - 1
+    for layer in range(last, 0, -1):
+        reducing, gathering = {}, {}
         for g in range(groups):
-            wide_grad = jnp.where(same_mol_t, nt(pick_t, pulled[layer, g * span : (g + 1) * span, :]), 0.0).astype(BF16)
-
-            def atoms_pair(ap, carry, g=g, wide_grad=wide_grad):
-                columns = pl.ds(pl.multiple_of(ap * 2 * width, 2 * width), 2 * width)
-                x = nn(wide_grad, sent[g * span : (g + 1) * span, columns])
-                where = pl.ds(pl.multiple_of(layer * rows_all + g * span + ap * 16, 16), 16)
-                for r in range(local):
-                    at = r * GROUP
-                    tile = jnp.concatenate([x[at : at + GROUP, :width], x[at : at + GROUP, width:]], axis=0)
-                    gt[where, r * width : (r + 1) * width] = tile.astype(BF16)
-                return carry
-
-            lax.fori_loop(0, atoms // 2, atoms_pair, 0, unroll=8)
-
+            gated_back(layer, g)
+            message_back(layer, g)
+            at = layer * rows_all + g * span
+            back = nn(gt[at : at + span, :], edge_low[...]).astype(BF16)
+            reduce_send[g * span : (g + 1) * span, :] = nn(order_back, back).astype(BF16)
+            reducing[g] = []
+            for k in range(1, ring):
+                rows = rows16(g * span + lax.rem(me + k, ring) * block, block)
+                stage = (LAYERS + 1) * groups + g
+                reducing[g].append(row_copy(stage, k, reduce_send.at[rows, :], reduce_recv.at[g, k - 1]))
+        gated_weights_back(layer)
+        for g in range(groups):
+            for copy in reducing[g]:
+                copy.wait_recv()
+            total = reduce_send[rows16(g * span + me * block, block), :].astype(F32)
+            for k in range(ring - 1):
+                total = total + reduce_recv[g, k].astype(F32)
+            parcels[LAYERS * groups + g, me] = total.astype(BF16)
+            gathering[g] = exchange(LAYERS * groups + g)
     rest_copies = []
-    for layer in reversed(range(LAYERS)):
-        gated_back(layer)
-        if layer == 0:
-            gated_weights_back(layer)
+    for g in range(groups):
+        for copy in gathering[g]:
+            copy.wait_recv()
+        for j in range(ring):
+            rows = slice(g * span + j * block, g * span + (j + 1) * block)
+            state_grad[rows, :] += parcels[LAYERS * groups + g, j].astype(F32)
+        gated_back(0, g)
+        if g == groups - 1:
+            gated_weights_back(0)
             for s in range(2):
                 for i in range(3):
                     at = (s * 3 + i) * width
@@ -499,27 +534,7 @@
                 peer = lax.rem(place + k, peers)
                 rows = rows16(peer * plan.rest_part, plan.rest_part)
                 rest_copies.append(far_copy(4, k - 1, peer, rest_part.at[rows, :], rest_recv.at[k - 1]))
-        message_back(layer)
-        if layer > 0:
-            back = nn(gt[layer * rows_all : (layer + 1) * rows_all, :], edge_low[...]).astype(BF16)
-            for g in range(groups):
-                reduce_send[g * span : (g + 1) * span, :] = nn(order_back, back[g * span : (g + 1) * span]).astype(BF16)
-            copies = []
-            for k in range(1, ring):
-                rows = rows16(lax.rem(me + k, ring) * block, block)
-                copies.append(row_copy(LAYERS + 1, k, reduce_send.at[rows, :], reduce_recv.at[k - 1]))
-            gated_weights_back(layer)
-            for copy in copies:
-                copy.wait_recv()
-            total = reduce_send[pl.ds(pl.multiple_of(me * block, block), block), :].astype(F32)
-            for k in range(ring - 1):
-                total = total + reduce_recv[k].astype(F32)
-            parcels[LAYERS, me] = total.astype(BF16)
-            for copy in exchange(LAYERS):
-                copy.wait_recv()
-            for j in range(ring):
-                rows = slice(j * block, (j + 1) * block)
-                state_grad[rows, :] += parcels[LAYERS, j].astype(F32)
+        message_back(0, g)
 
     for copy in head_copies:
         copy.wait_recv()
@@ -576,12 +591,7 @@
                 edge_copies.append(far_copy(3, k - 1, other * 2 + side, near_sum.at[rows, :], edge_recv.at[k - 1]))
 
     order_of = [*range(1, blocks), 0]
-    waiting = None
-    for j in order_of:
-        copies = scatter_near(j)
-        if waiting is not None:
-            scatter_far(*waiting)
-        waiting = (j, copies)
+    near_copies = [(j, scatter_near(j)) for j in order_of]
 
     def pair_grads(g):
         wide_grad = jnp.concatenate(
@@ -605,7 +615,8 @@
 
     for g in range(groups - 1):
         pair_grads(g)
-    scatter_far(*waiting)
+    for waiting in near_copies:
+        scatter_far(*waiting)
     for copy in rest_copies:
         copy.wait_recv()
     mine = rows16(place * plan.rest_part, plan.rest_part)
@@ -620,12 +631,12 @@
     for copy in head_copies:
         copy.wait_recv()
     rows = rows16(me * plan.head, plan.head)
-    head_rows = [row_copy(LAYERS + 2, k, head_all.at[rows, :], head_all.at[rows, :]) for k in range(1, ring)]
+    head_rows = [row_copy((LAYERS + 2) * groups, k, head_all.at[rows, :], head_all.at[rows, :]) for k in range(1, ring)]
     pair_grads(groups - 1)
 
     for copy in edge_copies:
         copy.wait_recv()
-    pieces = 2 if part >= WIDE else 1
+    pieces = plan.pieces
     size = part // pieces
     across, beside = {}, {}
     for p in range(pieces):
@@ -646,24 +657,23 @@
             rows = rows16((lax.rem(line - k + lines, lines) * 2 + side) * part + p * size, size)
             beside[p, k] = far_copy(5, p * peers + lines + k, neighbour, edge_all.at[rows, :], edge_all.at[rows, :])
 
-    lane_pair = iota((edges, atoms * atoms), 1).astype(F32)
-
-    def edge_back(m):
-        d_act = nn(one_hot(lane_pair == pair_cols[:, m : m + 1]), pair_grad[m])
-        d_first = d_act * slope[m]
-        return nn(feats[m], d_first.astype(BF16)), jnp.sum(d_first, axis=0, keepdims=True)
-
-    total_in, total_bias = edge_back(0)
-    for m in range(1, mols):
+    lane_pair = iota((edges // 2, atoms * atoms), 1).astype(F32)
+    total_bias = jnp.zeros((8, width), F32)
+    for m in range(mols):
         if m == mols // 2:
             for copy in rest_copies:
                 copy.wait_recv()
-            rest_rows = [row_copy(LAYERS + 3, k, rest_all.at[me], rest_all.at[me]) for k in range(1, ring)]
-        more_in, more_bias = edge_back(m)
-        total_in, total_bias = total_in + more_in, total_bias + more_bias
+            rest_rows = [row_copy((LAYERS + 2) * groups + 1, k, rest_all.at[me], rest_all.at[me]) for k in range(1, ring)]
+        for i in range(2):
+            rows = slice(i * edges // 2, (i + 1) * edges // 2)
+            d_first = nn(one_hot(lane_pair == pair_cols[rows, m : m + 1]), pair_grad[m]) * slope[m, rows, :]
+            total_bias = total_bias + jnp.sum(d_first.reshape(edges // 16, 8, width), axis=0)
+            first_grad[m * edges + i * edges // 2 : m * edges + (i + 1) * edges // 2, :] = d_first.astype(BF16)
+    total_in = nn(jnp.concatenate([feats[m] for m in range(mols)], axis=1), first_grad[...])
+    total_bias = jnp.sum(total_bias, axis=0, keepdims=True)
     first_row[me, 0:features, :] = total_in
     first_row[me, features : features + 8, :] = jnp.broadcast_to(total_bias, (8, width))
-    first_copies = [row_copy(LAYERS + 4, k, first_row.at[me], first_row.at[me]) for k in range(1, ring)]
+    first_copies = [row_copy((LAYERS + 2) * groups + 2, k, first_row.at[me], first_row.at[me]) for k in range(1, ring)]
     onward(0)
     for copy in first_copies:
         copy.wait_recv()
@@ -852,7 +862,8 @@
     ring = lax.axis_size("row")
     local = width // ring
     rows_all = mols * atoms
-    block = rows_all // ring
+    block = GROUP * atoms // ring
+    groups = mols // GROUP
     peers = lax.axis_size("mol")
     plan = Plan(ring, peers, width, local)
 
@@ -879,7 +890,6 @@
             pltpu.VMEM((mols // GROUP * LAYERS * GROUP * local, atoms * width), BF16),
             pltpu.VMEM((mols, edges, width), F32),
             pltpu.VMEM((mols, atoms * atoms, width), BF16),
-            pltpu.VMEM((LAYERS, rows_all, width), BF16),
             pltpu.VMEM((width, LAYERS * rows_all), BF16),
             pltpu.VMEM((LAYERS, rows_all, width), BF16),
             pltpu.VMEM((LAYERS, 4, rows_all, width), F32),
@@ -889,9 +899,9 @@
             pltpu.VMEM((LAYERS, rows_all, width), BF16),
             pltpu.VMEM((3 * width, 4 * width), BF16),
             pltpu.VMEM((width + 2 * mols, WIDE), F32),
-            pltpu.VMEM((LAYERS + 1, ring, block, WIDE), BF16),
+            pltpu.VMEM(((LAYERS + 1) * groups, ring, block, WIDE), BF16),
             pltpu.VMEM((rows_all, width), BF16),
-            pltpu.VMEM((ring - 1, block, width), BF16),
+            pltpu.VMEM((groups, ring - 1, block, width), BF16),
             pltpu.VMEM((2, width, 3 * width), F32),
             pltpu.VMEM((16, WIDE), F32),
             pltpu.VMEM((peers, 8, WIDE), F32),
@@ -905,10 +915,10 @@
             pltpu.VMEM((plan.rest, WIDE), BF16),
             pltpu.VMEM((peers - 1, plan.rest_part, WIDE), BF16),
             pltpu.VMEM((ring, plan.rest, WIDE), BF16),
-            pltpu.SemaphoreType.DMA((LAYERS + 5, ring - 1)),
-            pltpu.SemaphoreType.DMA((LAYERS + 5, ring - 1)),
-            pltpu.SemaphoreType.DMA((9, 2 * peers)),
-            pltpu.SemaphoreType.DMA((9, 2 * peers)),
+            pltpu.SemaphoreType.DMA(((LAYERS + 2) * groups + 3, ring - 1)),
+            pltpu.SemaphoreType.DMA(((LAYERS + 2) * groups + 3, ring - 1)),
+            pltpu.SemaphoreType.DMA((plan.stages[9],)),
+            pltpu.SemaphoreType.DMA((plan.stages[9],)),
             pltpu.VMEM((LAYERS * rows_all, local * width), BF16),
             pltpu.VMEM(edge_output.shape, F32),
             pltpu.VMEM(gated_weights.shape, F32),
@@ -920,6 +930,7 @@
             pltpu.VMEM((peers // 2 * plan.edge_part, WIDE), BF16),
             pltpu.VMEM((ring, features + 8, WIDE), F32),
             pltpu.VMEM((peers, features + 8, WIDE), F32),
+            pltpu.VMEM((mols * edges, width), BF16),
         ],
         compiler_params=pltpu.CompilerParams(
             collective_id=0, has_side_effects=True, vmem_limit_bytes=60 * 1024 * 1024

time: 104 us -> 96.4 us (0.927); the launches traced: 103 us -> 96.2 us
  Pallas kernels: 102 us -> 95.3 us
    pallas_call x1, Pallas kernels: 91 us -> 84.5 us  [shards(): pl.pallas_call(functools.partial(step_kernel, ring, peers), out_shape=[sh...]
where the time goes in v4:
time: 96.4 us; the launch traced here: 96.2 us
  Pallas kernels  95.3 us (99%)
    pallas_call x1, Pallas kernels, shards(): pl.pallas_call(functools.partial(step_kernel, ring, peers), out_shape=[sh...  84.5 us
    pallas_call x1, Pallas kernels, shards(): pl.pallas_call(functools.partial(update_kernel, ring, peers, local), out_...  10.8 us

profile of v4, /device:TPU:0, one launch (start us, length us, event | category | flops | bytes accessed | tf_op | source)
XLA Modules:
  0.0 96.2 jit_solution(3184707600009030156)
XLA Ops:
  0.7 84.5 %shard_map.508 = (bf16[4096,128]{1,0:T(8,128)(2,1)}, bf16[2048,128]{1,0:T(8,128)(2,1)}, bf16[4,256,128]{2,1,0:T(8,128)(2,1)}, f32[32,128]{1,0:T(8,128)}) custom-call(s32[16]{0:T(128)} %atom_counts.1, s32[16]{0:T(128)} %edge_counts.1, bf16[16,16,384]{2,1,0:T(8,128)(2,1)} %bitcast.11, s32[16,384]{1,0:T(8,128)} %source.1, s32[16,384]{1,0:T(8,128)} %target.1, ...), custom_call_target="tpu_custom_call" | custom-call | tf_op jit(solution)/shard_map/pallas_call | solution.py:875
  85.2 10.8 %shard_map.509 = (f32[1]{0:T(128)}, f32[1]{0:T(128)}, f32[16,128]{1,0:T(8,128)}, f32[16,128]{1,0:T(8,128)}, f32[16,128]{1,0:T(8,128)}, /*index=5*/bf16[16,128]{1...) custom-call(f32[32,128]{1,0:T(8,128)} %get-tuple-element.64.counted., ...), custom_call_target="tpu_custom_call" | custom-call | tf_op jit(solution)/shard_map/pallas_call | solution.py:961

commit v5 on v4

--- a/solution.py
+++ b/solution.py
@@ -201,7 +201,7 @@
     low_in = edge_in[...].astype(BF16)
 
     lane_edge = iota((1, edges), 1)
-    row_index = iota((256, edges), 0)
+    row_index = iota((atoms * atoms, edges), 0)
     for m in range(mols):
         pairs[m : m + 1, :] = jnp.where(
             lane_edge < edge_counts[m], source[m : m + 1, :] * atoms + target[m : m + 1, :], -1
@@ -218,11 +218,9 @@
         act = act.astype(BF16)
         pair = pairs[pl.ds(m, 1), :]
         rows = pl.ds(pl.multiple_of(m * atoms, atoms), atoms)
-        for part in range(atoms * atoms // 256):
-            sums = nn(one_hot(row_index + part * 256 == pair), act).astype(BF16)
-            for j in range(256 // atoms):
-                a = part * (256 // atoms) + j
-                sent[rows, a * width : (a + 1) * width] = sums[j * atoms : (j + 1) * atoms]
+        sums = nn(one_hot(row_index == pair), act).astype(BF16)
+        for a in range(atoms):
+            sent[rows, a * width : (a + 1) * width] = sums[a * atoms : (a + 1) * atoms]
         return carry
 
     lax.fori_loop(0, mols, edge_network, 0, unroll=4)
@@ -259,7 +257,7 @@
                 turned[where, a * width : (a + 1) * width] = tile.astype(BF16)
             return carry
 
-        lax.fori_loop(0, local // 2, rows_pair, 0, unroll=8)
+        lax.fori_loop(0, local // 2, rows_pair, 0, unroll=16)
         u = nt(sent[rows, :], turned[base : base + half, :])
         u = jnp.where(same_mol, u, 0.0).astype(BF16)
         packed = jnp.zeros((block, WIDE), F32)
@@ -484,7 +482,7 @@
                 gt[where, r * width : (r + 1) * width] = tile.astype(BF16)
             return carry
 
-        lax.fori_loop(0, atoms // 2, atoms_pair, 0, unroll=8)
+        lax.fori_loop(0, atoms // 2, atoms_pair, 0, unroll=16)
 
     last = LAYERS - 1
     for layer in range(last, 0, -1):
@@ -638,6 +636,13 @@
         copy.wait_recv()
     pieces = plan.pieces
     size = part // pieces
+    stores = []
+
+    def store(source_ref, target_ref):
+        copy = pltpu.make_async_copy(source_ref, target_ref, store_sem.at[len(stores)])
+        copy.start()
+        stores.append(copy)
+
     across, beside = {}, {}
     for p in range(pieces):
         own = rows16(line * part + p * size, size)
@@ -656,6 +661,7 @@
             across[p, k].wait_recv()
             rows = rows16((lax.rem(line - k + lines, lines) * 2 + side) * part + p * size, size)
             beside[p, k] = far_copy(5, p * peers + lines + k, neighbour, edge_all.at[rows, :], edge_all.at[rows, :])
+            store(edge_all.at[rows, :], edge_sum.at[rows, :])
 
     lane_pair = iota((edges // 2, atoms * atoms), 1).astype(F32)
     total_bias = jnp.zeros((8, width), F32)
@@ -688,13 +694,6 @@
     for p in range(1, pieces):
         onward(p)
 
-    stores = []
-
-    def store(source_ref, target_ref):
-        copy = pltpu.make_async_copy(source_ref, target_ref, store_sem.at[len(stores)])
-        copy.start()
-        stores.append(copy)
-
     for copy in head_rows:
         copy.wait_recv()
     store(head_all, head_sum)
@@ -709,9 +708,13 @@
         total_first = total_first + first_mol[k]
     totals[0:8, :] = total
     totals[8:, :] = total_first
-    for copy in beside.values():
-        copy.wait_recv()
-    store(edge_all, edge_sum)
+    for p in range(pieces):
+        rows = rows16(place * part + p * size, size)
+        store(edge_all.at[rows, :], edge_sum.at[rows, :])
+        for k in range(lines):
+            beside[p, k].wait_recv()
+            rows = rows16((lax.rem(line - k + lines, lines) * 2 + 1 - side) * part + p * size, size)
+            store(edge_all.at[rows, :], edge_sum.at[rows, :])
     for copy in started:
         copy.wait_send()
     for copy in stores:
@@ -726,7 +729,7 @@
     return (weight_new, first_new, second_new, weight_new.astype(BF16))
 
 
-PIECES = 4
+PIECES = 2
 
 
 def update_kernel(ring, peers, local, counted, totals, edge_far, head_far, rest_far, *refs):
@@ -925,7 +928,7 @@
             pltpu.VMEM(memory_weights.shape, F32),
             pltpu.VMEM(readout_hidden.shape, F32),
             pltpu.SemaphoreType.DMA((4,)),
-            pltpu.SemaphoreType.DMA((3,)),
+            pltpu.SemaphoreType.DMA((2 + plan.pieces * peers,)),
             pltpu.VMEM((peers // 2 * plan.edge_part, WIDE), BF16),
             pltpu.VMEM((peers // 2 * plan.edge_part, WIDE), BF16),
             pltpu.VMEM((ring, features + 8, WIDE), F32),

time: 96.4 us -> 93.8 us (0.973)
  Pallas kernels: 95.3 us -> 92.7 us
    pallas_call x1, Pallas kernels: 84.5 us -> 82.8 us  [shards(): pl.pallas_call(functools.partial(step_kernel, ring, peers), out_shape=[sh...]
where the time goes in v5:
time: 93.8 us; the launch traced here: 93.5 us
  Pallas kernels  92.7 us (99%)
    pallas_call x1, Pallas kernels, shards(): pl.pallas_call(functools.partial(step_kernel, ring, peers), out_shape=[sh...  82.8 us
    pallas_call x1, Pallas kernels, shards(): pl.pallas_call(functools.partial(update_kernel, ring, peers, local), out_...  9.89 us

profile of v5, /device:TPU:0, one launch (start us, length us, event | category | flops | bytes accessed | tf_op | source)
XLA Modules:
  0.0 93.5 jit_solution(16224468615909200325)
XLA Ops:
  0.7 82.8 %shard_map.508 = (bf16[4096,128]{1,0:T(8,128)(2,1)}, bf16[2048,128]{1,0:T(8,128)(2,1)}, bf16[4,256,128]{2,1,0:T(8,128)(2,1)}, f32[32,128]{1,0:T(8,128)}) custom-call(s32[16]{0:T(128)} %atom_counts.1, s32[16]{0:T(128)} %edge_counts.1, bf16[16,16,384]{2,1,0:T(8,128)(2,1)} %bitcast.11, s32[16,384]{1,0:T(8,128)} %source.1, s32[16,384]{1,0:T(8,128)} %target.1, ...), custom_call_target="tpu_custom_call" | custom-call | tf_op jit(solution)/shard_map/pallas_call | solution.py:878
  83.5 9.9 %shard_map.509 = (f32[1]{0:T(128)}, f32[1]{0:T(128)}, f32[16,128]{1,0:T(8,128)}, f32[16,128]{1,0:T(8,128)}, f32[16,128]{1,0:T(8,128)}, /*index=5*/bf16[16,128]{1...) custom-call(f32[32,128]{1,0:T(8,128)} %get-tuple-element.64.counted., ...), custom_call_target="tpu_custom_call" | custom-call | tf_op jit(solution)/shard_map/pallas_call | solution.py:964

commit v6 on v5

--- a/solution.py
+++ b/solution.py
@@ -743,8 +743,8 @@
     n_bias = olds[18].shape[0]
     plan = Plan(ring, peers, width, local)
     every = slice(None)
-    columns = plan.edge // PIECES
-    cuts = [(every, pl.ds(i * columns, columns)) for i in range(PIECES)]
+    depth = width // PIECES
+    cuts = [(pl.ds(i * depth, depth), every) for i in range(PIECES)]
     count = [0, 0]
 
     def copies_of(sides, sem, which):
@@ -786,9 +786,10 @@
     wait(edge_ready)
     for p in range(PIECES):
         wait(cut_ready[p])
-        for i in range(p * columns // width, (p + 1) * columns // width):
-            grad = edge_sum[i * width : (i + 1) * width, :].astype(F32) * inverse
-            update(1, (every, slice(i * width, (i + 1) * width)), grad)
+        for i in range(local):
+            at = i * width + p * depth
+            grad = edge_sum[at : at + depth, :].astype(F32) * inverse
+            update(1, (slice(p * depth, (p + 1) * depth), slice(i * width, (i + 1) * width)), grad)
         stored += store(1, cuts[p])
     wait(head_ready + ready[3])
     for i in range(4):

time: 93.8 us -> 93.6 us (level)
  no operation moved by 1% of the time
where the time goes in v6:
time: 93.6 us; the launch traced here: 93.4 us
  Pallas kernels  92.5 us (99%)
    pallas_call x1, Pallas kernels, shards(): pl.pallas_call(functools.partial(step_kernel, ring, peers), out_shape=[sh...  82.8 us
    pallas_call x1, Pallas kernels, shards(): pl.pallas_call(functools.partial(update_kernel, ring, peers, local), out_...  9.71 us

profile of v6, /device:TPU:0, one launch (start us, length us, event | category | flops | bytes accessed | tf_op | source)
XLA Modules:
  0.0 93.4 jit_solution(1402485898604070079)
XLA Ops:
  0.7 82.8 %shard_map.508 = (bf16[4096,128]{1,0:T(8,128)(2,1)}, bf16[2048,128]{1,0:T(8,128)(2,1)}, bf16[4,256,128]{2,1,0:T(8,128)(2,1)}, f32[32,128]{1,0:T(8,128)}) custom-call(s32[16]{0:T(128)} %atom_counts.1, s32[16]{0:T(128)} %edge_counts.1, bf16[16,16,384]{2,1,0:T(8,128)(2,1)} %bitcast.11, s32[16,384]{1,0:T(8,128)} %source.1, s32[16,384]{1,0:T(8,128)} %target.1, ...), custom_call_target="tpu_custom_call" | custom-call | tf_op jit(solution)/shard_map/pallas_call | solution.py:879
  83.5 9.7 %shard_map.509 = (f32[1]{0:T(128)}, f32[1]{0:T(128)}, f32[16,128]{1,0:T(8,128)}, f32[16,128]{1,0:T(8,128)}, f32[16,128]{1,0:T(8,128)}, /*index=5*/bf16[16,128]{1...) custom-call(f32[32,128]{1,0:T(8,128)} %get-tuple-element.64.counted., ...), custom_call_target="tpu_custom_call" | custom-call | tf_op jit(solution)/shard_map/pallas_call | solution.py:965
